TPU v7x, 32 devices: a whole 2x2x4 slice. The times are simulated.
32 devices in a mesh: frame: 8 (over y, x, core), batch: 4 (over z).
Axes of the slice: x: 2, y: 2, z: 4, core: 2. Of those that a mesh axis runs over, the one named last changes fastest.
Arguments:
- tokens: bfloat16 [16, 1024, 1024], P('batch', 'frame'), may hold values from -6 to 6
- out_cotangent: bfloat16 [16, 1024, 1024], P('batch', 'frame'), may hold values from -6 to 6
- buckets: int32 [16], P('batch'), may hold values from 0 to 1
- noise_levels: int32 [16, 4], P('batch'), may hold values from 0 to 999
- owned_block: int32 [32], replicated, may hold values from 0 to 31, as said below
- master: float32 [32, 589824], P(('frame', 'batch'))
- first_moment: float32 [32, 589824], P(('frame', 'batch'))
- second_moment: float32 [32, 589824], P(('frame', 'batch')), as said below
Outputs:
- activations: bfloat16 [16, 1024, 1024], P('batch', 'frame')
- input_grad: bfloat16 [16, 1024, 1024], P('batch', 'frame')
- new_master: float32 [32, 589824], P(('frame', 'batch'))
- new_first: float32 [32, 589824], P(('frame', 'batch'))
- new_second: float32 [32, 589824], P(('frame', 'batch'))
Inputs may be any that keep to these rules, and one draw needn't show every extreme that they name: `owned_block`: a permutation: every block of the flattened weights has exactly one owner. `second_moment`: positive.
All inputs are finite; a program needn't handle non-finite values.
Results may differ from a plain program's by a relative error of at most 0.012.
Values may be sent and summed in bfloat16 or wider, within the bound.
A program may use at most 448 MiB of HBM per device.

v0:
```python
from functools import partial
import math

import jax
import jax.numpy as jnp
from jax import lax
from jax.sharding import PartitionSpec as P

H = 16
HD = 64
FF = 4096
FRAME_LO = 256
STEP = 10


HIGHEST = lax.Precision.HIGHEST
NEG_FILL = -1e30
BETA_ONE = 0.5
BETA_TWO = 0.5
LEARN_RATE = 0.05
WEIGHT_DECAY = 0.1
ADAM_EPS = 1e-08


def layer_stats(values):
    centre = values - jnp.mean(values, axis=-1, keepdims=True)
    inv_std = lax.rsqrt(jnp.mean(centre * centre, axis=-1, keepdims=True) + 1e-06)
    return (centre * inv_std, inv_std)


def norm_back(upstream, normed, inv_std):
    mean_grad = jnp.mean(upstream, axis=-1, keepdims=True)
    mean_cross = jnp.mean(upstream * normed, axis=-1, keepdims=True)
    return inv_std * (upstream - mean_grad - normed * mean_cross)


def noise_embedding(levels, feature_width):
    half_width = feature_width // 2
    frequencies = jnp.exp(
        -math.log(10000.0) * jnp.arange(half_width, dtype=jnp.float32) / half_width
    )
    angles = levels.astype(jnp.float32)[:, None] * frequencies[None, :]
    return jnp.concatenate([jnp.cos(angles), jnp.sin(angles)], axis=1)


def split_flat(flat_values, model_width, hidden_width):
    matrix_shapes = (
        (model_width, 6 * model_width),
        (model_width, 3 * model_width),
        (model_width, model_width),
        (model_width, hidden_width),
        (hidden_width, model_width),
    )
    matrices = []
    offset_now = 0
    for matrix_shape in matrix_shapes:
        entry_count = matrix_shape[0] * matrix_shape[1]
        matrices.append(flat_values[offset_now : offset_now + entry_count].reshape(matrix_shape))
        offset_now = offset_now + entry_count
    return matrices


def fold_keys(carry, piece, q_heads, frame_end):
    key_rows, value_rows = piece
    row_count = key_rows.shape[0]
    step_rows = math.gcd(row_count, 512)
    block_count = row_count // step_rows
    heads = q_heads.shape[1]
    head_size = q_heads.shape[2]
    key_blocks = key_rows.reshape(block_count, step_rows, heads, head_size)
    value_blocks = value_rows.reshape(block_count, step_rows, heads, head_size)

    def one_block(state, block_args):
        running_max, running_sum, partial_out = state
        key_block, value_block, first_row = block_args
        scores = jnp.einsum("qhd,khd->hqk", q_heads, key_block, preferred_element_type=jnp.float32)
        visible = (first_row + jnp.arange(step_rows, dtype=jnp.int32))[None, None, :] < frame_end[
            None, :, None
        ]
        scores = jnp.where(visible, scores, NEG_FILL)
        new_max = jnp.maximum(running_max, jnp.max(scores, axis=-1))
        weights = jnp.where(visible, jnp.exp(scores - new_max[..., None]), 0.0)
        fade = jnp.exp(running_max - new_max)
        running_sum = running_sum * fade + jnp.sum(weights, axis=-1)
        gained = jnp.einsum(
            "hqk,khd->qhd",
            weights.astype(jnp.bfloat16),
            value_block,
            preferred_element_type=jnp.float32,
        )
        partial_out = partial_out * jnp.transpose(fade)[:, :, None] + gained
        return ((new_max, running_sum, partial_out), None)

    first_rows = jnp.arange(block_count, dtype=jnp.int32) * step_rows
    carry, unused = lax.scan(one_block, carry, (key_blocks, value_blocks, first_rows))
    return carry


def shards(
    tokens, out_cotangent, buckets, noise_levels, owned_block, master, first_moment, second_moment
):
    micro_count, tok_count, model_width = tokens.shape
    heads = H
    head_size = HD
    hidden_width = FF
    block_size = master.shape[1]
    frame_count = noise_levels.shape[1]
    seq_len = tok_count * lax.axis_size("frame")
    q_scale = head_size ** (-0.5)
    row_total = micro_count * tok_count
    gathered = lax.all_gather(master.astype(jnp.bfloat16), ("frame", "batch"), axis=0, tiled=True)
    placed = jnp.take(gathered, jnp.argsort(owned_block), axis=0).reshape(-1)
    w_ada, w_qkv, w_out, w_in, w_down = split_flat(placed, model_width, hidden_width)
    positions = lax.axis_index("frame") * tok_count + jnp.arange(tok_count, dtype=jnp.int32)
    frame_len = FRAME_LO * (1 + 3 * buckets)
    frame_of = positions[None, :] // frame_len[:, None]
    frame_end = (frame_of + 1) * frame_len[:, None]
    silu_cond = jax.nn.silu(
        jax.vmap(lambda level_row: noise_embedding(level_row, model_width))(noise_levels)
    ).astype(jnp.bfloat16)
    modulation = jnp.einsum("mfd,de->mfe", silu_cond, w_ada, preferred_element_type=jnp.float32)
    selector = (
        frame_of[:, :, None] == jnp.arange(frame_count, dtype=jnp.int32)[None, None, :]
    ).astype(jnp.float32)
    token_mod = jnp.einsum("mtf,mfe->mte", selector, modulation, precision=HIGHEST).reshape(
        row_total, 6 * model_width
    )
    shift_one, scale_one, gate_one, shift_two, scale_two, gate_two = jnp.split(token_mod, 6, axis=1)
    x_float = tokens.reshape(row_total, model_width).astype(jnp.float32)
    normed_one, inv_one = layer_stats(x_float)
    h_one = (normed_one * (1.0 + scale_one) + shift_one).astype(jnp.bfloat16)
    projected = jnp.dot(h_one, w_qkv, preferred_element_type=jnp.float32)
    queries = (projected[:, :model_width] * q_scale).astype(jnp.bfloat16)
    key_part = projected[:, model_width : 2 * model_width].astype(jnp.bfloat16)
    value_part = projected[:, 2 * model_width :].astype(jnp.bfloat16)
    q_all = queries.reshape(micro_count, tok_count, heads, head_size)
    key_micro = key_part.reshape(micro_count, tok_count, model_width)
    value_micro = value_part.reshape(micro_count, tok_count, model_width)
    head_list = []
    total_list = []
    for micro in range(micro_count):
        q_heads = q_all[micro]
        ends = frame_end[micro]
        start_state = (
            jnp.full((heads, tok_count), NEG_FILL, jnp.float32),
            jnp.zeros((heads, tok_count), jnp.float32),
            jnp.zeros((tok_count, heads, head_size), jnp.float32),
        )

        def fold_local(state, piece, start, q_heads=q_heads, ends=ends):
            key_rows, value_rows = piece
            shaped = (
                key_rows.reshape(key_rows.shape[0], heads, head_size),
                value_rows.reshape(value_rows.shape[0], heads, head_size),
            )
            return fold_keys(state, shaped, q_heads, ends)

        running_max, running_sum, partial_out = fold_local(
            start_state,
            (
                lax.all_gather(key_micro[micro], "frame", axis=0, tiled=True),
                lax.all_gather(value_micro[micro], "frame", axis=0, tiled=True),
            ),
            jnp.int32(0),
        )
        head_list.append(partial_out / jnp.transpose(running_sum)[:, :, None])
        total_list.append(running_max + jnp.log(running_sum))
    attn_heads = jnp.stack(head_list)
    attended = attn_heads.reshape(row_total, model_width).astype(jnp.bfloat16)
    attn_out = jnp.dot(attended, w_out, preferred_element_type=jnp.float32)
    middle = x_float + gate_one * attn_out
    normed_two, inv_two = layer_stats(middle)
    h_two = (normed_two * (1.0 + scale_two) + shift_two).astype(jnp.bfloat16)
    pre_act = jnp.dot(h_two, w_in, preferred_element_type=jnp.float32)
    activated, gelu_back = jax.vjp(partial(jax.nn.gelu, approximate=True), pre_act)
    act_low = activated.astype(jnp.bfloat16)
    mlp_out = jnp.dot(act_low, w_down, preferred_element_type=jnp.float32)
    block_output = (middle + gate_two * mlp_out).astype(jnp.bfloat16)
    grad_out = out_cotangent.reshape(row_total, model_width).astype(jnp.float32)
    d_mlp = (gate_two * grad_out).astype(jnp.bfloat16)
    g_down = jnp.dot(act_low.T, d_mlp, preferred_element_type=jnp.float32)
    d_act = jnp.dot(d_mlp, w_down.T, preferred_element_type=jnp.float32)
    d_pre = gelu_back(d_act)[0].astype(jnp.bfloat16)
    g_in = jnp.dot(h_two.T, d_pre, preferred_element_type=jnp.float32)
    d_htwo = jnp.dot(d_pre, w_in.T, preferred_element_type=jnp.float32)
    d_gate_two = grad_out * mlp_out
    d_scale_two = d_htwo * normed_two
    d_middle = grad_out + norm_back(d_htwo * (1.0 + scale_two), normed_two, inv_two)
    d_attn = (gate_one * d_middle).astype(jnp.bfloat16)
    d_gate_one = d_middle * attn_out
    g_out = jnp.dot(attended.T, d_attn, preferred_element_type=jnp.float32)
    d_attended = jnp.dot(d_attn, w_out.T, preferred_element_type=jnp.float32).astype(jnp.bfloat16)
    d_heads_all = d_attended.reshape(micro_count, tok_count, heads, head_size)
    step_rows = math.gcd(seq_len, 512)
    block_count = seq_len // step_rows
    first_rows = jnp.arange(block_count, dtype=jnp.int32) * step_rows
    dq_list = []
    dk_list = []
    dv_list = []
    for micro in range(micro_count):
        q_heads = q_all[micro]
        ends = frame_end[micro]
        log_total = total_list[micro]
        d_heads = d_heads_all[micro]
        row_dot = jnp.transpose(jnp.sum(d_heads.astype(jnp.float32) * attn_heads[micro], axis=-1))
        back_keys, back_values = (
            lax.all_gather(key_micro[micro], "frame", axis=0, tiled=True),
            lax.all_gather(value_micro[micro], "frame", axis=0, tiled=True),
        )
        key_blocks = back_keys.reshape(block_count, step_rows, heads, head_size)
        value_blocks = back_values.reshape(block_count, step_rows, heads, head_size)

        def back_block(
            dq_total,
            block_args,
            q_heads=q_heads,
            ends=ends,
            log_total=log_total,
            d_heads=d_heads,
            row_dot=row_dot,
        ):
            key_block, value_block, first_row = block_args
            scores = jnp.einsum(
                "qhd,khd->hqk", q_heads, key_block, preferred_element_type=jnp.float32
            )
            visible = (first_row + jnp.arange(step_rows, dtype=jnp.int32))[None, None, :] < ends[
                None, :, None
            ]
            probability = jnp.where(visible, jnp.exp(scores - log_total[..., None]), 0.0)
            d_values = jnp.einsum(
                "hqk,qhd->khd",
                probability.astype(jnp.bfloat16),
                d_heads,
                preferred_element_type=jnp.float32,
            )
            d_probs = jnp.einsum(
                "qhd,khd->hqk", d_heads, value_block, preferred_element_type=jnp.float32
            )
            d_scores = (probability * (d_probs - row_dot[..., None])).astype(jnp.bfloat16)
            dq_total = dq_total + jnp.einsum(
                "hqk,khd->qhd", d_scores, key_block, preferred_element_type=jnp.float32
            )
            d_keys = jnp.einsum(
                "hqk,qhd->khd", d_scores, q_heads, preferred_element_type=jnp.float32
            )
            return (
                dq_total,
                jnp.concatenate(
                    [
                        d_keys.reshape(step_rows, model_width),
                        d_values.reshape(step_rows, model_width),
                    ],
                    axis=1,
                ),
            )

        dq_sum, key_grads = lax.scan(
            back_block,
            jnp.zeros((tok_count, heads, head_size), jnp.float32),
            (key_blocks, value_blocks, first_rows),
        )
        own_grads = lax.psum_scatter(
            key_grads.reshape(seq_len, 2 * model_width).astype(jnp.bfloat16),
            "frame",
            scatter_dimension=0,
            tiled=True,
        ).astype(jnp.float32)
        dk_list.append(own_grads[:, :model_width].astype(jnp.bfloat16))
        dv_list.append(own_grads[:, model_width:].astype(jnp.bfloat16))
        dq_list.append(
            dq_sum.reshape(tok_count, model_width).astype(jnp.bfloat16) * jnp.bfloat16(q_scale)
        )
    d_proj = jnp.concatenate(
        [
            jnp.concatenate(dq_list, axis=0),
            jnp.concatenate(dk_list, axis=0),
            jnp.concatenate(dv_list, axis=0),
        ],
        axis=1,
    )
    g_qkv = jnp.dot(h_one.T, d_proj, preferred_element_type=jnp.float32)
    d_hone = jnp.dot(d_proj, w_qkv.T, preferred_element_type=jnp.float32)
    d_scale_one = d_hone * normed_one
    d_input = d_middle + norm_back(d_hone * (1.0 + scale_one), normed_one, inv_one)
    d_token_mod = jnp.concatenate(
        [d_hone, d_scale_one, d_gate_one, d_htwo, d_scale_two, d_gate_two], axis=1
    ).reshape(micro_count, tok_count, 6 * model_width)
    d_frame_mod = jnp.einsum("mtf,mte->mfe", selector, d_token_mod, precision=HIGHEST)
    g_ada = jnp.einsum("mfd,mfe->de", silu_cond.astype(jnp.float32), d_frame_mod, precision=HIGHEST)
    flat_grads = jnp.concatenate(
        [grad_piece.reshape(-1) for grad_piece in (g_ada, g_qkv, g_out, g_in, g_down)]
    )
    arranged = jnp.take(flat_grads.reshape(-1, block_size), owned_block, axis=0).reshape(-1)
    shard_total = lax.psum_scatter(
        arranged, ("frame", "batch"), scatter_dimension=0, tiled=True
    ).reshape(1, block_size)
    new_first = BETA_ONE * first_moment + (1.0 - BETA_ONE) * shard_total
    new_second = BETA_TWO * second_moment + (1.0 - BETA_TWO) * shard_total * shard_total
    fix_one = 1.0 - BETA_ONE**STEP
    fix_two = 1.0 - BETA_TWO**STEP
    update = new_first / fix_one / (jnp.sqrt(new_second / fix_two) + ADAM_EPS)
    new_master = master - LEARN_RATE * (update + WEIGHT_DECAY * master)
    outputs = block_output.reshape(micro_count, tok_count, model_width)
    input_grads = d_input.astype(jnp.bfloat16).reshape(micro_count, tok_count, model_width)
    return (outputs, input_grads, new_master, new_first, new_second)


def solution(mesh):
    placed = (
        P("batch", "frame", None),
        P("batch", "frame", None),
        P("batch"),
        P("batch", None),
        P(),
        P(("frame", "batch"), None),
        P(("frame", "batch"), None),
        P(("frame", "batch"), None),
    )
    return jax.shard_map(
        shards,
        mesh=mesh,
        in_specs=placed,
        out_specs=(
            P("batch", "frame", None),
            P("batch", "frame", None),
            P(("frame", "batch"), None),
            P(("frame", "batch"), None),
            P(("frame", "batch"), None),
        ),
        check_vma=False,
    )
```

profile of v0, /device:TPU:0, one launch (start us, length us, event | category | flops | bytes accessed | tf_op | source)
XLA Modules:
  0.0 2933.1 jit_solution(14636605072105200413)
XLA Ops:
  20.1 391.9 %all-gather.27.cloned.1.call-done = bf16[32,1,589824]{2,1,0:T(2,128)(2,1)} async-done(((bf16[1,1,589824]{2,1,0:T(2,128)(2,1)}), bf16[32,1,589824]{2,1,0:T(2,128)(2,1)}) %all-gather.27.cloned.1.call-update) | async-done | bytes 37748752 | tf_op jit(solution)/shard_map/all_gather | solution.py:111
  411.9 64.8 %copy.391 = bf16[32,1,589824]{2,0,1:T(8,128)(2,1)} copy(bf16[32,1,589824]{2,1,0:T(2,128)(2,1)} %all-gather.27.cloned.1.call-done) | data formatting | bytes 75497472
  483.4 20.7 fusion.252
  504.1 19.2 gather_fusion.3
  630.0 46.2 %gather.18 = bf16[6144,3072]{1,0:T(8,128)(2,1)} reshape(bf16[32,589824]{1,0:T(8,128)(2,1)} %constant_dynamic-update-slice_fusion.4) | data formatting | bytes 75497472 | tf_op jit(solution)/shard_map/jit(_take)/gather | solution.py:112
  676.2 46.2 %gather.17 = bf16[3072,6144]{1,0:T(8,128)(2,1)} reshape(bf16[32,589824]{1,0:T(8,128)(2,1)} %constant_dynamic-update-slice_fusion.4) | data formatting | bytes 75497472 | tf_op jit(solution)/shard_map/jit(_take)/gather | solution.py:112
  754.7 46.6 %gather.20 = bf16[4608,4096]{1,0:T(8,128)(2,1)} reshape(bf16[32,589824]{1,0:T(8,128)(2,1)} %constant_dynamic-update-slice_fusion.4) | data formatting | bytes 75497472 | tf_op jit(solution)/shard_map/jit(_take)/gather | solution.py:112
  801.3 46.6 %gather.19 = bf16[18432,1024]{1,0:T(8,128)(2,1)} reshape(bf16[32,589824]{1,0:T(8,128)(2,1)} %constant_dynamic-update-slice_fusion.4) | data formatting | bytes 75497472 | tf_op jit(solution)/shard_map/jit(_take)/gather | solution.py:112
  850.6 25.8 broadcast_select_fusion
  1094.6 31.7 %while.116 = (s32[]{:T(128)}, f32[128,16,64]{0,2,1:T(8,128)S(1)}, bf16[2,512,2048]{2,1,0:T(8,128)(2,1)}, bf16[2,512,16,64]{1,3,2,0:T(8,128)(2,1)}, s32[2]{0:T(12...) while((s32[]{:T(128)}, f32[128,16,64]{0,2,1:T(8,128)S(1)}, ...), condition=%wide.region_25.26_spmd.clone, body=%wide.region_24.25_spmd.clone.sunk | while | flops 683999744 | bytes 39023276 | solution.py:257
  1130.3 33.0 %while.119 = (s32[]{:T(128)}, f32[128,16,64]{0,2,1:T(8,128)}, bf16[2,512,2048]{2,1,0:T(8,128)(2,1)}, bf16[2,512,16,64]{1,3,2,0:T(8,128)(2,1)}, s32[2]{0:T(128)S(...) while((s32[]{:T(128)}, f32[128,16,64]{0,2,1:T(8,128)}, ...), condition=%wide.region_34.35_spmd.clone, body=%wide.region_33.34_spmd.clone.sunk | while | flops 683999744 | bytes 39023276 | solution.py:257
  1167.1 32.0 %while.118 = (s32[]{:T(128)}, f32[128,16,64]{0,2,1:T(8,128)S(1)}, bf16[2,512,2048]{2,1,0:T(8,128)(2,1)}, bf16[2,512,16,64]{1,3,2,0:T(8,128)(2,1)}, s32[2]{0:T(12...) while((s32[]{:T(128)}, f32[128,16,64]{0,2,1:T(8,128)S(1)}, ...), condition=%wide.region_31.32_spmd.clone, body=%wide.region_30.31_spmd.clone.sunk | while | flops 683999744 | bytes 39023276 | solution.py:257
  1203.1 31.3 %while.117 = (s32[]{:T(128)}, f32[128,16,64]{0,2,1:T(8,128)S(1)}, bf16[2,512,2048]{2,1,0:T(8,128)(2,1)}, bf16[2,512,16,64]{1,3,2,0:T(8,128)(2,1)}, s32[2]{0:T(12...) while((s32[]{:T(128)}, f32[128,16,64]{0,2,1:T(8,128)S(1)}, ...), condition=%wide.region_28.29_spmd.clone, body=%wide.region_27.28_spmd.clone.sunk | while | flops 683999744 | bytes 39023276 | solution.py:257
  1288.3 52.4 %reduce-scatter.15.cloned.1.call-done = bf16[128,2048]{1,0:T(8,128)(2,1)} async-done(((bf16[1024,2048]{1,0:T(8,128)(2,1)}), bf16[128,2048]{1,0:T(8,128)(2,1)}) %reduce-scatter.15.cloned.1.call-update) | async-done | bytes 524304
  1458.0 64.3 %reshape.672 = f32[32,589824]{1,0:T(8,128)} reshape(f32[18874368]{0:T(1024)} %constant_dynamic-update-slice_fusion.18) | data formatting | bytes 150994944 | tf_op jit(solution)/shard_map/reshape | solution.py:293
  1533.9 39.8 %fusion.251 = (f32[32,118016]{1,0:T(8,128)}, f32[32,118016]{1,0:T(8,128)}, f32[32,118016]{1,0:T(8,128)}, f32[32,118016]{1,0:T(8,128)}) fusion(f32[32,589824]{1,0:T(8,128)} %reshape.672), kind=kLoop, calls=%fused_computation.397 | loop fusion | bytes 120848384 | tf_op jit(solution)/shard_map/jit(_take)/gather | solution.py:293
  1573.7 21.5 gather_fusion.8
  1595.2 21.8 gather_fusion.9
  1617.1 21.6 gather_fusion.7
  1638.7 21.8 gather_fusion.6
  1660.4 21.8 gather_fusion.5
  1740.3 49.7 %select_bitcast_fusion = f32[4,4608,8,128]{3,2,1,0:T(8,128)} fusion(f32[32,589824]{1,0:T(8,128)} %constant_dynamic-update-slice_fusion.13, pred[32]{0:T(512)(128)(4,1)S(1)} %copy-done.93), kind=kLoop, calls=%fused_computation.226 | loop fusion | flops 18874368 | bytes 150994976
  1790.0 49.7 %copy.375 = f32[4,4608,8,128]{3,1,2,0:T(8,128)} copy(f32[4,4608,8,128]{3,2,1,0:T(8,128)} %select_bitcast_fusion) | data formatting | bytes 150994944
  1839.7 1069.2 %all-reduce.3.cloned.1.call-done = f32[18874368]{0:T(1024)} async-done(((f32[18874368]{0:T(1024)}), f32[18874368]{0:T(1024)}) %all-reduce.3.cloned.1.call-update) | async-done | bytes 75497488
  (596 shorter events, 830.6 us)
Async XLA Ops:
  7.2 404.7 %all-gather.27.cloned.1.call-start = ((), (), s32[]{:S(2)}) async-start(), calls=%async_computation.12 | async-start | bytes 77856768 | tf_op jit(solution)/shard_map/all_gather | solution.py:111
  12.6 863.9 %all-gather.11.cloned.1.call-start = ((), (), s32[]{:S(2)}) async-start(), calls=%async_computation.4 | async-start | bytes 2359296 | tf_op jit(solution)/shard_map/all_gather | solution.py:161
  676.2 46.2 %copy-start.92 = (pred[1024]{0:T(1024)(128)(4,1)S(1)}, pred[1024]{0:T(1024)(128)(4,1)}, u32[]{:S(2)}) copy-start(pred[1024]{0:T(1024)(128)(4,1)} %slice.213) | copy-start | bytes 3076
  749.8 138.7 %all-gather.15.cloned.1.call-start = ((), (), s32[]{:S(2)}) async-start(), calls=%async_computation.6 | async-start | bytes 2359296 | tf_op jit(solution)/shard_map/all_gather | solution.py:161
  750.5 149.8 %all-gather.17.cloned.1.call-start = ((), (), s32[]{:S(2)}) async-start(), calls=%async_computation.7 | async-start | bytes 2359296 | tf_op jit(solution)/shard_map/all_gather | solution.py:162
  751.1 175.2 %all-gather.19.cloned.1.call-start = ((), (), s32[]{:S(2)}) async-start(), calls=%async_computation.8 | async-start | bytes 2359296 | tf_op jit(solution)/shard_map/all_gather | solution.py:161
  751.7 186.8 %all-gather.21.cloned.1.call-start = ((), (), s32[]{:S(2)}) async-start(), calls=%async_computation.9 | async-start | bytes 2359296 | tf_op jit(solution)/shard_map/all_gather | solution.py:162
  752.2 212.4 %all-gather.23.cloned.1.call-start = ((), (), s32[]{:S(2)}) async-start(), calls=%async_computation.10 | async-start | bytes 2359296 | tf_op jit(solution)/shard_map/all_gather | solution.py:161
  753.0 223.8 %all-gather.25.cloned.1.call-start = ((), (), s32[]{:S(2)}) async-start(), calls=%async_computation.11 | async-start | bytes 2359296 | tf_op jit(solution)/shard_map/all_gather | solution.py:162
  850.5 152.3 %all-gather.13.cloned.1.call-start = ((), (), s32[]{:S(2)}) async-start(), calls=%async_computation.5 | async-start | bytes 2359296 | tf_op jit(solution)/shard_map/all_gather | solution.py:162
  876.4 393.8 %reduce-scatter.13.cloned.1.call-start = ((), (), s32[]{:S(2)}) async-start(), calls=%async_computation.13 | async-start | bytes 4718592
  926.2 103.5 %copy-start.40 = (f32[128,16,64]{0,2,1:T(8,128)}, f32[128,16,64]{0,2,1:T(8,128)S(1)}, u32[]{:S(2)}) copy-start(f32[128,16,64]{0,2,1:T(8,128)S(1)} %get-tuple-element.437) | copy-start | bytes 1572868
  926.2 103.5 %copy-start.58 = (f32[16,128]{1,0:T(8,128)}, f32[16,128]{1,0:T(8,128)S(1)}, u32[]{:S(2)}) copy-start(f32[16,128]{1,0:T(8,128)S(1)} %get-tuple-element.438) | copy-start | bytes 24580
  964.6 65.3 %copy-start.38 = (f32[128,16,64]{0,2,1:T(8,128)}, f32[128,16,64]{0,2,1:T(8,128)S(1)}, u32[]{:S(2)}) copy-start(f32[128,16,64]{0,2,1:T(8,128)S(1)} %get-tuple-element.439) | copy-start | bytes 1572868
  964.6 65.3 %copy-start.56 = (f32[16,128]{1,0:T(8,128)}, f32[16,128]{1,0:T(8,128)S(1)}, u32[]{:S(2)}) copy-start(f32[16,128]{1,0:T(8,128)S(1)} %get-tuple-element.440) | copy-start | bytes 24580
  1126.4 145.3 %reduce-scatter.19.cloned.1.call-start = ((), (), s32[]{:S(2)}) async-start(), calls=%async_computation.16 | async-start | bytes 4718592
  1163.3 122.2 %reduce-scatter.17.cloned.1.call-start = ((), (), s32[]{:S(2)}) async-start(), calls=%async_computation.15 | async-start | bytes 4718592
  1199.2 141.5 %reduce-scatter.15.cloned.1.call-start = ((), (), s32[]{:S(2)}) async-start(), calls=%async_computation.14 | async-start | bytes 4718592
  1234.4 1674.5 %all-reduce.3.cloned.1.call-start = ((), (), s32[]{:S(2)}) async-start(), calls=%async_computation.17 | async-start | bytes 150994944
  1270.1 73.3 %copy-start.12 = (bf16[4,128,1024]{2,1,0:T(8,128)(2,1)S(1)}, bf16[4,128,1024]{2,1,0:T(8,128)(2,1)}, u32[]{:S(2)}) copy-start(bf16[4,128,1024]{2,1,0:T(8,128)(2,1)} %param.24) | copy-start | bytes 3145732
  1270.1 73.3 %copy-start.79 = (f32[512]{0:T(512)S(1)}, f32[512]{0:T(512)}, u32[]{:S(2)}) copy-start(f32[512]{0:T(512)} %get-tuple-element.1352) | copy-start | bytes 6148
  1270.1 73.2 %copy-start.81 = (f32[512]{0:T(512)S(1)}, f32[512]{0:T(512)}, u32[]{:S(2)}) copy-start(f32[512]{0:T(512)} %rsqrt_bitcast_fusion) | copy-start | bytes 6148
  1270.1 73.2 %copy-start.90 = (pred[1024]{0:T(1024)(128)(4,1)S(1)}, pred[1024]{0:T(1024)(128)(4,1)}, u32[]{:S(2)}) copy-start(pred[1024]{0:T(1024)(128)(4,1)} %slice.215) | copy-start | bytes 3076
  1839.7 1071.4 %copy-start.20 = (f32[1,589824]{1,0:T(1,128)S(1)}, f32[1,589824]{1,0:T(1,128)}, u32[]{:S(2)}) copy-start(f32[1,589824]{1,0:T(1,128)} %param.29) | copy-start | bytes 7077892
  (100 other events, 858.8 us)
Sparse Core Ops, SparseCore 0:
  12.7 399.1 all-gather.26
  749.9 26.0 all-gather.10
  778.5 27.8 all-gather.14
  808.7 27.8 all-gather.16
  838.9 27.8 all-gather.18
  868.6 27.8 all-gather.20
  898.4 27.8 all-gather.22
  928.2 27.8 all-gather.24
  958.1 27.8 all-gather.12
  1126.5 49.2 reduce-scatter.12
  1179.5 51.3 reduce-scatter.18
  1234.2 51.2 reduce-scatter.16
  1289.2 51.3 reduce-scatter.14
  1839.8 1069.0 all-reduce.2
where the time goes:
time: 2940 us; the launch traced here: 2930 us
  waiting for transfers between devices  1530 us (52%)
  local copies, waits for them, and re-layouts  1000 us (34%)
  matrix products  234 us (8%)
  other arithmetic  148 us (5%)
    unnamed x19, waiting for transfers between devices  1140 us
    all_gather x1, waiting for transfers between devices, shards(): lax.all_gather(master.astype(jnp.bfloat16), ('frame', 'batch'), axis=0, t...  392 us
    unnamed x259, local copies, waits for them, and re-layouts  347 us
    gather x11, local copies, waits for them, and re-layouts, shards(): placed = jnp.take(gathered, jnp.argsort(owned_block), axis=0).reshape(-1)  308 us
    gather x7, local copies, waits for them, and re-layouts, shards(): jnp.take(flat_grads.reshape(-1, block_size), owned_block, axis=0)  160 us
    reshape x1, local copies, waits for them, and re-layouts, shards(): flat_grads.reshape(-1, block_size)  64.3 us
  transfers between devices with their start and end apart: 14, of which 4 were waited for; matrix products, arithmetic and copies ran while one was open for 14% of the time, Pallas kernels for 0%

commit v1 on v0

v1 whole, which is shorter than its diff:
```python
from functools import partial
import math

import jax
import jax.numpy as jnp
import numpy as np
from jax import lax
from jax.experimental import pallas as pl
from jax.experimental.pallas import tpu as pltpu
from jax.sharding import PartitionSpec as P

H = 16
HD = 64
FF = 4096
FRAME_LO = 256
STEP = 10

HIGHEST = lax.Precision.HIGHEST
NEG_FILL = -1e30
BETA_ONE = 0.5
BETA_TWO = 0.5
LEARN_RATE = 0.05
WEIGHT_DECAY = 0.1
ADAM_EPS = 1e-08
MESH = pl.DeviceIdType.MESH
F32 = jnp.float32
BF16 = jnp.bfloat16
ANY = pl.BlockSpec(memory_space=pl.ANY)
VMEM_LIMIT = 60 * 1024 * 1024

ROWS = 576
GROUP = 144
FIRST = 10
KINDS = (("qkv", 1024, 3), ("out", 1024, 1), ("in", 1024, 4), ("down", 4096, 1))
SPANS = {"qkv": (96, 864), "out": (864, 1120), "in": (1120, 2144), "down": (2144, 3168)}
HELD = 3168


def pieces(kind, z):
    if kind == "qkv":
        found = [(96 + 16 * j, 16, 16 * z, j) for j in range(3)]
        for k in range(5):
            found += [(144 + 144 * k + 48 * j, 48, 64 + 192 * k + 48 * z, j) for j in range(3)]
        return found
    if kind == "out":
        return [(864, 144, 144 * z, 0), (1008, 112, 576 + 112 * z, 0)]
    if kind == "in":
        return [(1120, 1024, 0, z)]
    found = [(2144, 16, 16 * z, 0)]
    return found + [(2160 + 144 * k, 144, 64 + 576 * k + 144 * z, 0) for k in range(7)]


def block_rows(block):
    t = np.arange(GROUP)
    groups = []
    for z in range(4):
        if block == 10:
            i = t - 96
            rows = np.where(t < 96, 96 * z + t, 384 + 3 * (16 * z + i % 16) + i // 16)
        elif 11 <= block <= 15:
            rows = 3 * (48 * z + t % 48) + t // 48
        elif block == 17:
            rows = np.where(t < 112, 112 * z + t, 448 + 4 * (t - 112) + z)
        elif 18 <= block <= 23:
            rows = 4 * t + z
        elif block == 24:
            rows = np.where(t < 128, 4 * t + z, 512 + 16 * z + t - 128)
        else:
            rows = GROUP * z + t
        groups.append(rows)
    return np.concatenate(groups)


def ada_rows(z):
    t = jnp.arange(GROUP, dtype=jnp.int32)
    rows = [96 * b + 24 * z + t // 6 for b in range(10)]
    rows.append(jnp.where(t < 96, 960 + 16 * z + t // 6, -1))
    return jnp.concatenate(rows), jnp.tile(t % 6, 11)


def frame_index():
    return lax.axis_index("frame"), lax.axis_index("batch")


def strip_of(f):
    return 4 * (f % 2) + f // 2


def greet(devices):
    barrier = pltpu.get_barrier_semaphore()
    for device in devices:
        pl.semaphore_signal(barrier, inc=1, device_id=device, device_id_type=MESH)
    pl.semaphore_wait(barrier, len(devices))


def greet_all(total, batch):
    f, z = frame_index()
    me = f * batch + z
    barrier = pltpu.get_barrier_semaphore()

    def hail(k, carry):
        other = (me + k) % total
        pl.semaphore_signal(barrier, inc=1, device_id=(other // batch, other % batch), device_id_type=MESH)
        return carry

    lax.fori_loop(1, total, hail, 0)
    pl.semaphore_wait(barrier, total - 1)


def remote(src, dst, send, recv, device):
    copy = pltpu.make_async_remote_copy(
        src_ref=src, dst_ref=dst, send_sem=send, recv_sem=recv, device_id=device, device_id_type=MESH
    )
    copy.start()
    return copy


def local(src, dst, sem):
    copy = pltpu.make_async_copy(src, dst, sem)
    copy.start()
    return copy


def video_kernel(videos, per, arrays, *refs):
    ins, outs = refs[:arrays], refs[arrays : 2 * arrays]
    send, recv, own = refs[2 * arrays :]
    f, z = frame_index()
    mine, g = f // per, f % per
    others = [((mine + k) % videos, k) for k in range(1, videos)]
    greet([(v * per + g, z) for v, k in others])
    copies = []
    for a in range(arrays):
        for v, k in others:
            copies.append(
                remote(ins[a].at[v], outs[a].at[mine], send.at[a, k], recv.at[a, k], (v * per + g, z))
            )
        copies.append(local(ins[a].at[mine], outs[a].at[mine], own.at[a]))
    for copy in copies:
        copy.wait()


def swap_videos(arrays, videos, per, ident):
    count = len(arrays)
    return pl.pallas_call(
        partial(video_kernel, videos, per, count),
        out_shape=[jax.ShapeDtypeStruct(a.shape, a.dtype) for a in arrays],
        in_specs=[ANY] * count,
        out_specs=[ANY] * count,
        scratch_shapes=[
            pltpu.SemaphoreType.DMA((count, videos)),
            pltpu.SemaphoreType.DMA((count, videos)),
            pltpu.SemaphoreType.DMA((count,)),
        ],
        compiler_params=pltpu.CompilerParams(collective_id=ident, has_side_effects=True),
        name="swap_videos",
    )(*arrays)


def scatter_kernel(total, batch, blk, levels, tok, cot, cut, all_levels, tok_out, cot_out, send, recv, vsend, vrecv, lsend, lrecv, own):
    f, z = frame_index()
    me = f * batch + z
    greet_all(total, batch)
    mine, g = f // 2, f % 2

    def group(k, start):
        other = (me + k) % total
        of, oz = other // batch, other % batch
        copy = pltpu.make_async_remote_copy(
            src_ref=blk.at[pl.ds(pl.multiple_of(GROUP * oz, 16), GROUP), pl.ds(pl.multiple_of(128 * strip_of(of), 128), 128)],
            dst_ref=cut.at[me],
            send_sem=send.at[k],
            recv_sem=recv.at[k],
            device_id=(of, oz),
            device_id_type=MESH,
        )
        if start:
            copy.start()
        else:
            copy.wait()

    copies = []
    for k in range(1, batch):
        copies.append(remote(levels, all_levels.at[z], lsend.at[k], lrecv.at[k], (f, (z + k) % batch)))
    copies.append(local(levels, all_levels.at[z], own.at[0]))
    lax.fori_loop(1, total, lambda k, c: (group(k, True), c)[1], 0)
    copies.append(
        local(
            blk.at[pl.ds(pl.multiple_of(GROUP * z, 16), GROUP), pl.ds(pl.multiple_of(128 * strip_of(f), 128), 128)],
            cut.at[me],
            own.at[1],
        )
    )
    for a, (src, dst) in enumerate(((tok, tok_out), (cot, cot_out))):
        for k in range(1, 4):
            v = (mine + k) % 4
            copies.append(remote(src.at[v], dst.at[mine], vsend.at[a, k], vrecv.at[a, k], (v * 2 + g, z)))
        copies.append(local(src.at[mine], dst.at[mine], own.at[2 + a]))
    for copy in copies:
        copy.wait()
    lax.fori_loop(1, total, lambda k, c: (group(k, False), c)[1], 0)


def scatter_blocks(blk, levels, tok, cot, total, batch):
    return pl.pallas_call(
        partial(scatter_kernel, total, batch),
        out_shape=[
            jax.ShapeDtypeStruct((total, GROUP, 128), BF16),
            jax.ShapeDtypeStruct((batch,) + levels.shape, levels.dtype),
            jax.ShapeDtypeStruct(tok.shape, tok.dtype),
            jax.ShapeDtypeStruct(cot.shape, cot.dtype),
        ],
        in_specs=[ANY] * 4,
        out_specs=[ANY] * 4,
        scratch_shapes=[
            pltpu.SemaphoreType.DMA((total,)),
            pltpu.SemaphoreType.DMA((total,)),
            pltpu.SemaphoreType.DMA((2, 4)),
            pltpu.SemaphoreType.DMA((2, 4)),
            pltpu.SemaphoreType.DMA((batch,)),
            pltpu.SemaphoreType.DMA((batch,)),
            pltpu.SemaphoreType.DMA((4,)),
        ],
        compiler_params=pltpu.CompilerParams(collective_id=0, has_side_effects=True),
        name="scatter_blocks",
    )(blk, levels, tok, cot)


def collect_kernel(total, batch, cut, act, grad, blk, act_out, grad_out, send, recv, vsend, vrecv, own):
    f, z = frame_index()
    me = f * batch + z
    greet_all(total, batch)
    mine, g = f // 2, f % 2

    def spot(of, oz):
        return blk.at[pl.ds(pl.multiple_of(GROUP * oz, 16), GROUP), pl.ds(pl.multiple_of(128 * strip_of(of), 128), 128)]

    def group(k, start):
        other = (me + k) % total
        copy = pltpu.make_async_remote_copy(
            src_ref=cut.at[other],
            dst_ref=spot(f, z),
            send_sem=send.at[k],
            recv_sem=recv.at[k],
            device_id=(other // batch, other % batch),
            device_id_type=MESH,
        )
        if start:
            copy.start()
        else:
            copy.wait()

    lax.fori_loop(1, total, lambda k, c: (group(k, True), c)[1], 0)
    copies = [local(cut.at[me], spot(f, z), own.at[0])]
    for a, (src, dst) in enumerate(((act, act_out), (grad, grad_out))):
        for k in range(1, 4):
            v = (mine + k) % 4
            copies.append(remote(src.at[v], dst.at[mine], vsend.at[a, k], vrecv.at[a, k], (v * 2 + g, z)))
        copies.append(local(src.at[mine], dst.at[mine], own.at[1 + a]))
    for copy in copies:
        copy.wait()
    lax.fori_loop(1, total, lambda k, c: (group(k, False), c)[1], 0)


def collect_blocks(cut, act, grad, total, batch):
    return pl.pallas_call(
        partial(collect_kernel, total, batch),
        out_shape=[
            jax.ShapeDtypeStruct((ROWS, 1024), BF16),
            jax.ShapeDtypeStruct(act.shape, act.dtype),
            jax.ShapeDtypeStruct(grad.shape, grad.dtype),
        ],
        in_specs=[ANY] * 3,
        out_specs=[ANY] * 3,
        scratch_shapes=[
            pltpu.SemaphoreType.DMA((total,)),
            pltpu.SemaphoreType.DMA((total,)),
            pltpu.SemaphoreType.DMA((2, 4)),
            pltpu.SemaphoreType.DMA((2, 4)),
            pltpu.SemaphoreType.DMA((3,)),
        ],
        compiler_params=pltpu.CompilerParams(collective_id=3, has_side_effects=True),
        name="collect_blocks",
    )(cut, act, grad)


def plane():
    f, z = frame_index()
    y, x, c = f // 4, (f // 2) % 2, f % 2
    at_x = (4 * y + 2 * (1 - x) + c, z)
    at_y = (4 * (1 - y) + 2 * x + c, z)
    at_c = (4 * y + 2 * x + 1 - c, z)
    return y, x, c, z, at_x, at_y, at_c


def lanes(first, count):
    return pl.ds(pl.multiple_of(first, 128), count)


def gather_kernel(total, batch, held, mod, *refs):
    mats = dict(zip([kind for kind, _, _ in KINDS], refs[:4]))
    mod_out, zsend, zrecv, psend, precv, msend, mrecv, own = refs[4:]
    y, x, c, z, at_x, at_y, at_c = plane()
    f = 4 * y + 2 * x + c
    me = f * batch + z
    strip = 4 * c + 2 * y + x
    greet_all(total, batch)

    def mod_group(k, start):
        other = (me + k) % total
        of, oz = other // batch, other % batch
        copy = pltpu.make_async_remote_copy(
            src_ref=mod.at[4 * oz + of // 2],
            dst_ref=mod_out.at[z, :, lanes(128 * strip, 128)],
            send_sem=msend.at[k],
            recv_sem=mrecv.at[k],
            device_id=(of, oz),
            device_id_type=MESH,
        )
        if start:
            copy.start()
        else:
            copy.wait()

    sends = []
    for m, (kind, _, _) in enumerate(KINDS):
        for k in range(1, batch):
            for row, count, to, j in pieces(kind, z):
                src = held.at[pl.ds(row, count)]
                dst = mats[kind].at[pl.ds(pl.multiple_of(to, 16), count), lanes(1024 * j + 128 * strip, 128)]
                remote(src, dst, zsend.at[m, k], zrecv.at[m, k], (f, (z + k) % batch))
        for row, count, to, j in pieces(kind, z):
            local(
                held.at[pl.ds(row, count)],
                mats[kind].at[pl.ds(pl.multiple_of(to, 16), count), lanes(1024 * j + 128 * strip, 128)],
                own.at[m],
            )
        if m == 0:
            lax.fori_loop(1, total, lambda k, cc: (mod_group(k, True), cc)[1], 0)
    mod_own = local(mod.at[4 * z + f // 2], mod_out.at[z, :, lanes(128 * strip, 128)], own.at[4])

    def whole(m):
        lo, hi = SPANS[KINDS[m][0]]
        return held.at[pl.ds(lo, hi - lo)]

    def z_wait(m):
        for k in range(1, batch):
            pltpu.make_async_copy(whole(m), whole(m), zrecv.at[m, k]).wait()
        pltpu.make_async_copy(whole(m), whole(m), own.at[m]).wait()

    slots = {}
    counter = [0]

    def push(key, mat, row, count, col, width, device):
        s = counter[0]
        counter[0] += 1
        ref = mat.at[pl.ds(row, count), lanes(col, width)]
        slots.setdefault(key, []).append(remote(ref, ref, psend.at[s], precv.at[s], device))

    def first(m):
        kind, depth, blocks = KINDS[m]
        half = depth // 2
        for j in range(blocks):
            push((m, 1), mats[kind], 0, half, 1024 * j + 128 * strip, 128, at_x)
            push((m, 1), mats[kind], half, half, 1024 * j + 128 * strip, 128, at_y)

    def second(m):
        kind, depth, blocks = KINDS[m]
        half = depth // 2
        for copy in slots[(m, 1)]:
            copy.wait_recv()
        for j in range(blocks):
            push((m, 2), mats[kind], 0, half, 1024 * j + 512 * c + 256 * y, 256, at_y)
            for yy in range(2):
                push((m, 2), mats[kind], half, half, 1024 * j + 512 * c + 256 * yy + 128 * x, 128, at_x)

    def third(m):
        kind, depth, blocks = KINDS[m]
        for copy in slots[(m, 2)]:
            copy.wait_recv()
        for j in range(blocks):
            push((m, 3), mats[kind], 0, depth, 1024 * j + 512 * c, 512, at_c)

    z_wait(0)
    first(0)
    z_wait(1)
    first(1)
    second(0)
    z_wait(2)
    first(2)
    second(1)
    third(0)
    z_wait(3)
    first(3)
    second(2)
    third(1)
    second(3)
    third(2)
    third(3)
    for m in range(4):
        for copy in slots[(m, 3)]:
            copy.wait_recv()
    for copies in slots.values():
        for copy in copies:
            copy.wait_send()
    for m in range(4):
        for k in range(1, batch):
            pltpu.make_async_copy(whole(m), whole(m), zsend.at[m, k]).wait()
    mod_own.wait()
    lax.fori_loop(1, total, lambda k, cc: (mod_group(k, False), cc)[1], 0)


def gather_matrices(held, mod, total, batch):
    return pl.pallas_call(
        partial(gather_kernel, total, batch),
        out_shape=[jax.ShapeDtypeStruct((depth, 1024 * blocks), BF16) for _, depth, blocks in KINDS]
        + [jax.ShapeDtypeStruct((batch, mod.shape[1], 1024), F32)],
        in_specs=[ANY] * 2,
        out_specs=[ANY] * 5,
        scratch_shapes=[
            pltpu.SemaphoreType.DMA((4, batch)),
            pltpu.SemaphoreType.DMA((4, batch)),
            pltpu.SemaphoreType.DMA((54,)),
            pltpu.SemaphoreType.DMA((54,)),
            pltpu.SemaphoreType.DMA((total,)),
            pltpu.SemaphoreType.DMA((total,)),
            pltpu.SemaphoreType.DMA((5,)),
        ],
        compiler_params=pltpu.CompilerParams(collective_id=1, has_side_effects=True),
        name="gather_matrices",
    )(held, mod)


def add_rows(dst, dst_col, src, src_col, width, first, count):
    step = 128

    def body(i, carry):
        rows = pl.ds(pl.multiple_of(first + i * step, 16), step)
        dst[rows, lanes(dst_col, width)] = dst[rows, lanes(dst_col, width)] + src[rows, lanes(src_col, width)]
        return carry

    lax.fori_loop(0, count // step, body, 0)


ORDER = (3, 2, 1, 0)


def reduce_kernel(total, batch, *refs):
    grads, dmod, out, dmod_out = refs[:4], refs[4], refs[5], refs[6]
    own, got, half_sum, strip_sum = refs[7:11], refs[11:15], refs[15:19], refs[19:23]
    zgot, psend, precv, lsem, zsend, zrecv, msend, mrecv, mown = refs[23:]
    y, x, c, z, at_x, at_y, at_c = plane()
    f = 4 * y + 2 * x + c
    me = f * batch + z
    greet_all(total, batch)

    def mod_group(k, start):
        other = (me + k) % total
        of, oz = other // batch, other % batch
        copy = pltpu.make_async_remote_copy(
            src_ref=dmod.at[:, lanes(128 * strip_of(of), 128)],
            dst_ref=dmod_out.at[me],
            send_sem=msend.at[k],
            recv_sem=mrecv.at[k],
            device_id=(of, oz),
            device_id_type=MESH,
        )
        if start:
            copy.start()
        else:
            copy.wait()

    slots = {}
    counter = [0]

    def push(key, src, dst, device):
        s = counter[0]
        counter[0] += 1
        slots.setdefault(key, []).append(remote(src, dst, psend.at[s], precv.at[s], device))

    def arrive(key):
        for copy in slots[key]:
            copy.wait_recv()

    def zero(m):
        kind, depth, blocks = KINDS[m]
        for j in range(blocks):
            push((m, 0), grads[m].at[:, lanes(1024 * j + 512 * (1 - c), 512)], got[m].at[:, lanes(512 * j, 512)], at_c)
        loads[m] = [
            local(grads[m].at[:, lanes(1024 * j + 512 * c, 512)], own[m].at[:, lanes(512 * j, 512)], lsem.at[m, j])
            for j in range(blocks)
        ]

    def first(m):
        kind, depth, blocks = KINDS[m]
        half = depth // 2
        for copy in loads[m]:
            copy.wait()
        arrive((m, 0))
        add_rows(own[m], 0, got[m], 0, 512 * blocks, 0, depth)
        for j in range(blocks):
            for yy in range(2):
                push(
                    (m, 1),
                    own[m].at[pl.ds(0, half), lanes(512 * j + 256 * yy + 128 * (1 - x), 128)],
                    half_sum[m].at[pl.ds(0, half), lanes(256 * j + 128 * yy, 128)],
                    at_x,
                )
            push(
                (m, 1),
                own[m].at[pl.ds(half, half), lanes(512 * j + 256 * (1 - y), 256)],
                half_sum[m].at[pl.ds(half, half), lanes(256 * j, 256)],
                at_y,
            )

    def second(m):
        kind, depth, blocks = KINDS[m]
        half = depth // 2
        arrive((m, 1))
        for j in range(blocks):
            for yy in range(2):
                add_rows(half_sum[m], 256 * j + 128 * yy, own[m], 512 * j + 256 * yy + 128 * x, 128, 0, half)
            add_rows(half_sum[m], 256 * j, own[m], 512 * j + 256 * y, 256, half, half)
        for j in range(blocks):
            push(
                (m, 2),
                half_sum[m].at[pl.ds(0, half), lanes(256 * j + 128 * (1 - y), 128)],
                strip_sum[m].at[pl.ds(0, half), lanes(128 * j, 128)],
                at_y,
            )
            push(
                (m, 2),
                half_sum[m].at[pl.ds(half, half), lanes(256 * j + 128 * (1 - x), 128)],
                strip_sum[m].at[pl.ds(half, half), lanes(128 * j, 128)],
                at_x,
            )

    def third(m):
        kind, depth, blocks = KINDS[m]
        half = depth // 2
        arrive((m, 2))
        for j in range(blocks):
            add_rows(strip_sum[m], 128 * j, half_sum[m], 256 * j + 128 * y, 128, 0, half)
            add_rows(strip_sum[m], 128 * j, half_sum[m], 256 * j + 128 * x, 128, half, half)
        for k in range(1, batch):
            to = (z + k) % batch
            for row, count, at, j in pieces(kind, to):
                remote(
                    strip_sum[m].at[pl.ds(pl.multiple_of(at, 16), count), lanes(128 * j, 128)],
                    zgot.at[k - 1, pl.ds(row, count)],
                    zsend.at[m, k],
                    zrecv.at[m, k],
                    (f, to),
                )

    def whole(m, k):
        lo, hi = SPANS[KINDS[m][0]]
        return zgot.at[k - 1, pl.ds(lo, hi - lo)]

    def last(m):
        kind, depth, blocks = KINDS[m]
        for k in range(1, batch):
            pltpu.make_async_copy(whole(m, k), whole(m, k), zrecv.at[m, k]).wait()
        for row, count, at, j in pieces(kind, z):
            step = 128 if count == 1024 else count

            def body(i, carry, row=row, at=at, j=j, step=step):
                rows = pl.ds(pl.multiple_of(row + i * step, 16), step)
                mine = strip_sum[m][pl.ds(pl.multiple_of(at + i * step, 16), step), lanes(128 * j, 128)]
                total_sum = mine.astype(F32)
                for k in range(batch - 1):
                    total_sum = total_sum + zgot[k, rows, :].astype(F32)
                out[rows, :] = total_sum.astype(BF16)
                return carry

            lax.fori_loop(0, count // step, body, 0)

    loads = {}
    a, b, cc, d = ORDER
    zero(a)
    zero(b)
    zero(cc)
    zero(d)
    lax.fori_loop(1, total, lambda k, u: (mod_group(k, True), u)[1], 0)
    mod_own = local(dmod.at[:, lanes(128 * strip_of(f), 128)], dmod_out.at[me], mown)
    out[pl.ds(0, 96), :] = jnp.zeros((96, 128), BF16)
    first(a)
    first(b)
    second(a)
    first(cc)
    second(b)
    third(a)
    first(d)
    second(cc)
    third(b)
    second(d)
    last(a)
    third(cc)
    last(b)
    third(d)
    last(cc)
    last(d)
    for copies in slots.values():
        for copy in copies:
            copy.wait_send()
    for m in range(4):
        for k in range(1, batch):
            pltpu.make_async_copy(whole(m, k), whole(m, k), zsend.at[m, k]).wait()
    mod_own.wait()
    lax.fori_loop(1, total, lambda k, u: (mod_group(k, False), u)[1], 0)


def reduce_matrices(grads, dmod, total, batch):
    def bufs(width):
        return [pltpu.VMEM((depth, blocks * width), BF16) for _, depth, blocks in KINDS]

    return pl.pallas_call(
        partial(reduce_kernel, total, batch),
        out_shape=[
            jax.ShapeDtypeStruct((HELD, 128), BF16),
            jax.ShapeDtypeStruct((total, dmod.shape[0], 128), F32),
        ],
        in_specs=[ANY] * 5,
        out_specs=[pl.BlockSpec(memory_space=pltpu.VMEM), ANY],
        scratch_shapes=bufs(512)
        + bufs(512)
        + bufs(256)
        + bufs(128)
        + [
            pltpu.VMEM((batch - 1, HELD, 128), BF16),
            pltpu.SemaphoreType.DMA((54,)),
            pltpu.SemaphoreType.DMA((54,)),
            pltpu.SemaphoreType.DMA((4, 4)),
            pltpu.SemaphoreType.DMA((4, batch)),
            pltpu.SemaphoreType.DMA((4, batch)),
            pltpu.SemaphoreType.DMA((total,)),
            pltpu.SemaphoreType.DMA((total,)),
            pltpu.SemaphoreType.DMA,
        ],
        compiler_params=pltpu.CompilerParams(
            collective_id=2, has_side_effects=True, vmem_limit_bytes=VMEM_LIMIT
        ),
        name="reduce_matrices",
    )(*grads, dmod)


def pick_kernel(index, src, dst):
    def body(i, carry):
        dst[i] = src[index[i]]
        return carry

    lax.fori_loop(0, dst.shape[0], body, 0)


def pick_blocks(index, src):
    whole = pl.BlockSpec(memory_space=pltpu.VMEM)
    return pl.pallas_call(
        pick_kernel,
        out_shape=jax.ShapeDtypeStruct((index.shape[0],) + src.shape[1:], src.dtype),
        in_specs=[pl.BlockSpec(memory_space=pltpu.SMEM), whole],
        out_specs=whole,
        name="pick_blocks",
    )(index, src)


def key_positions(rows, piece, per):
    i = lax.broadcasted_iota(jnp.int32, (rows, 1), 0)
    local_rows = rows // per
    return ((i % local_rows) // piece * per + i // local_rows) * piece + i % piece


def scores_t(k, q, ends, piece, per):
    s = lax.dot_general(k, q, (((1,), (1,)), ((), ())), preferred_element_type=F32)
    pos = key_positions(k.shape[0], piece, per)
    cols = []
    for t in range(q.shape[0] // piece):
        part = s[:, t * piece : (t + 1) * piece]
        cols.append(jnp.where(pos < ends[t], part, NEG_FILL))
    return jnp.concatenate(cols, axis=1)


def attend_kernel(piece, per, ends, q, k, v, o):
    outs = []
    for a in range(2):
        cut = slice(64 * a, 64 * a + 64)
        s = scores_t(k[:, cut], q[:, cut], ends, piece, per)
        peak = jnp.max(s, axis=0, keepdims=True)
        e = jnp.exp(s - peak)
        p = (e * (1.0 / jnp.sum(e, axis=0, keepdims=True))).astype(BF16)
        outs.append(lax.dot_general(p, v[:, cut], (((0,), (0,)), ((), ())), preferred_element_type=F32))
    o[...] = jnp.concatenate(outs, axis=1).astype(BF16)


def attend(ends, q, kv, piece, per):
    rows, width = q.shape
    keys = kv.shape[0]
    pairs = width // 128
    return pl.pallas_call(
        partial(attend_kernel, piece, per),
        grid_spec=pltpu.PrefetchScalarGridSpec(
            num_scalar_prefetch=1,
            grid=(pairs,),
            in_specs=[
                pl.BlockSpec((rows, 128), lambda h, e: (0, h)),
                pl.BlockSpec((keys, 128), lambda h, e: (0, h)),
                pl.BlockSpec((keys, 128), lambda h, e: (0, h + pairs)),
            ],
            out_specs=pl.BlockSpec((rows, 128), lambda h, e: (0, h)),
        ),
        out_shape=jax.ShapeDtypeStruct((rows, width), BF16),
        compiler_params=pltpu.CompilerParams(vmem_limit_bytes=VMEM_LIMIT),
        cost_estimate=pl.CostEstimate(
            flops=4 * rows * keys * width, bytes_accessed=4 * (rows + keys) * width, transcendentals=rows * keys * H
        ),
        name="attend",
    )(ends, q, kv, kv)


def attend_back_kernel(piece, per, ends, q, k, v, do, dq, dk, dv):
    dqs, dks, dvs = [], [], []
    for a in range(2):
        cut = slice(64 * a, 64 * a + 64)
        qa, ka, va, da = q[:, cut], k[:, cut], v[:, cut], do[:, cut]
        s = scores_t(ka, qa, ends, piece, per)
        peak = jnp.max(s, axis=0, keepdims=True)
        e = jnp.exp(s - peak)
        p = e * (1.0 / jnp.sum(e, axis=0, keepdims=True))
        dvs.append(jnp.dot(p.astype(BF16), da, preferred_element_type=F32))
        dp = lax.dot_general(va, da, (((1,), (1,)), ((), ())), preferred_element_type=F32)
        pdp = p * dp
        row = jnp.sum(pdp, axis=0, keepdims=True)
        ds = (pdp - p * row).astype(BF16)
        dks.append(jnp.dot(ds, qa, preferred_element_type=F32))
        dqs.append(lax.dot_general(ds, ka, (((0,), (0,)), ((), ())), preferred_element_type=F32))
    dq[...] = jnp.concatenate(dqs, axis=1).astype(BF16)
    dk[...] = jnp.concatenate(dks, axis=1).astype(BF16)
    dv[...] = jnp.concatenate(dvs, axis=1).astype(BF16)


def attend_back(ends, q, kv, do, piece, per):
    rows, width = q.shape
    keys = kv.shape[0]
    pairs = width // 128
    mine = pl.BlockSpec((rows, 128), lambda h, e: (0, h))
    allk = pl.BlockSpec((keys, 128), lambda h, e: (0, h))
    return pl.pallas_call(
        partial(attend_back_kernel, piece, per),
        grid_spec=pltpu.PrefetchScalarGridSpec(
            num_scalar_prefetch=1,
            grid=(pairs,),
            in_specs=[mine, allk, pl.BlockSpec((keys, 128), lambda h, e: (0, h + pairs)), mine],
            out_specs=[mine, allk, allk],
        ),
        out_shape=[
            jax.ShapeDtypeStruct((rows, width), BF16),
            jax.ShapeDtypeStruct((keys, width), BF16),
            jax.ShapeDtypeStruct((keys, width), BF16),
        ],
        compiler_params=pltpu.CompilerParams(vmem_limit_bytes=VMEM_LIMIT),
        cost_estimate=pl.CostEstimate(
            flops=10 * rows * keys * width, bytes_accessed=6 * (rows + keys) * width, transcendentals=rows * keys * H
        ),
        name="attend_back",
    )(ends, q, kv, kv, do)


def layer_stats(values):
    centre = values - jnp.mean(values, axis=-1, keepdims=True)
    inv_std = lax.rsqrt(jnp.mean(centre * centre, axis=-1, keepdims=True) + 1e-06)
    return (centre * inv_std, inv_std)


def norm_back(upstream, normed, inv_std):
    mean_grad = jnp.mean(upstream, axis=-1, keepdims=True)
    mean_cross = jnp.mean(upstream * normed, axis=-1, keepdims=True)
    return inv_std * (upstream - mean_grad - normed * mean_cross)


def noise_embedding(levels, feature_width):
    half_width = feature_width // 2
    frequencies = jnp.exp(
        -math.log(10000.0) * jnp.arange(half_width, dtype=jnp.float32) / half_width
    )
    angles = levels.astype(jnp.float32)[:, None] * frequencies[None, :]
    return jnp.concatenate([jnp.cos(angles), jnp.sin(angles)], axis=1)


def silu_embedding(levels, width):
    return jax.nn.silu(noise_embedding(levels, width)).astype(BF16)


def split_flat(flat_values, model_width, hidden_width):
    matrix_shapes = (
        (model_width, 6 * model_width),
        (model_width, 3 * model_width),
        (model_width, model_width),
        (model_width, hidden_width),
        (hidden_width, model_width),
    )
    matrices = []
    offset_now = 0
    for matrix_shape in matrix_shapes:
        entry_count = matrix_shape[0] * matrix_shape[1]
        matrices.append(flat_values[offset_now : offset_now + entry_count].reshape(matrix_shape))
        offset_now = offset_now + entry_count
    return matrices


def shards(
    frame_size,
    batch_size,
    tokens,
    out_cotangent,
    buckets,
    noise_levels,
    owned_block,
    master,
    first_moment,
    second_moment,
):
    micro_count, piece, width = tokens.shape
    block_size = master.shape[1]
    frame_count = noise_levels.shape[1]
    total = frame_size * batch_size
    videos = micro_count
    per = frame_size // videos
    rows = videos * piece
    keys = rows * per
    q_scale = HD ** (-0.5)
    f, z = frame_index()
    me = f * batch_size + z
    mine, g = f // per, f % per
    direct = frame_size == 8 and batch_size == 4 and block_size == ROWS * 1024 and videos == 4 and frame_count == 4

    if direct:
        inverse = jnp.argsort(owned_block).astype(jnp.int32)
        table = jnp.asarray(np.stack([block_rows(b) for b in range(total)]).astype(np.int32))
        own_rows = lax.dynamic_index_in_dim(table, owned_block[me], 0, keepdims=False)
        swap = (own_rows[:, None] == jnp.arange(ROWS, dtype=jnp.int32)[None, :]).astype(BF16)
        cut_block = jnp.dot(swap, master.reshape(ROWS, 1024).astype(BF16), preferred_element_type=F32).astype(BF16)
        levels = jnp.zeros((8, 128), jnp.int32).at[:4, :4].set(noise_levels)
        cut, all_levels, tok, cot = scatter_blocks(cut_block, levels, tokens, out_cotangent, total, batch_size)
        ordered = pick_blocks(inverse, cut)
        held = ordered[FIRST:].reshape(HELD, 128)
        cond = silu_embedding(all_levels[:, :4, :4].reshape(64), width)
        ada_row, ada_col = ada_rows(z)
        spread = (ada_row[None, :] == jnp.arange(width, dtype=jnp.int32)[:, None]).astype(BF16)
        cond_rows = jnp.dot(cond, spread, preferred_element_type=F32).astype(BF16)
        six = (ada_col[None, :] == jnp.arange(6, dtype=jnp.int32)[:, None]).astype(BF16)
        cond_all = (cond_rows.reshape(16, 1, 4, -1) * six[None, :, None, :]).reshape(384, -1)
        mod_part = jnp.dot(
            cond_all, ordered[: FIRST + 1].reshape(-1, 128), preferred_element_type=F32
        ).reshape(16, 24, 128)
        w_qkv, w_out, w_in, w_down, mod_parts = gather_matrices(held, mod_part, total, batch_size)
        modulation = jnp.sum(mod_parts, axis=0).reshape(6, 4, width).transpose(1, 0, 2)
    else:
        tok, cot = swap_videos([tokens, out_cotangent], videos, per, 0)
        gathered = lax.all_gather(master.astype(BF16), ("frame", "batch"), axis=0, tiled=True)
        placed = jnp.take(gathered, jnp.argsort(owned_block), axis=0).reshape(-1)
        w_ada, w_qkv, w_out, w_in, w_down = split_flat(placed, width, FF)
        cond = silu_embedding(lax.dynamic_index_in_dim(noise_levels, mine, 0, keepdims=False), width)
        modulation = jnp.dot(cond, w_ada, preferred_element_type=F32).reshape(frame_count, 6, width)

    frame_len = FRAME_LO * (1 + 3 * buckets[mine])
    piece_at = (jnp.arange(videos, dtype=jnp.int32) * per + g) * piece
    piece_frame = piece_at // frame_len
    ends = (piece_frame + 1) * frame_len
    selector = (piece_frame[:, None] == jnp.arange(frame_count, dtype=jnp.int32)[None, :]).astype(F32)
    piece_mod = jnp.einsum("pf,fjd->jpd", selector, modulation, precision=HIGHEST)
    shift_one, scale_one, gate_one, shift_two, scale_two, gate_two = [piece_mod[j][:, None, :] for j in range(6)]

    def flat(a):
        return a.reshape(rows, a.shape[-1])

    def cube(a):
        return a.reshape(videos, piece, a.shape[-1])

    x_float = tok.astype(F32)
    normed_one, inv_one = layer_stats(x_float)
    h_one = flat((normed_one * (1.0 + scale_one) + shift_one).astype(BF16))
    projected = jnp.dot(h_one, w_qkv, preferred_element_type=F32)
    queries = (projected[:, :width] * q_scale).astype(BF16)
    kv_own = projected[:, width:].astype(BF16)

    def partners(k):
        return [(i, i // per * per + (i + k) % per) for i in range(frame_size)]

    kv_all = jnp.zeros((per, rows, 2 * width), BF16)
    kv_all = lax.dynamic_update_index_in_dim(kv_all, kv_own, g, 0)
    for k in range(1, per):
        kv_all = lax.dynamic_update_index_in_dim(
            kv_all, lax.ppermute(kv_own, "frame", partners(k)), (g + per - k) % per, 0
        )
    kv_all = kv_all.reshape(keys, 2 * width)
    attended = attend(ends, queries, kv_all, piece, per)
    attn_out = jnp.dot(attended, w_out, preferred_element_type=F32)
    middle = x_float + gate_one * cube(attn_out)
    normed_two, inv_two = layer_stats(middle)
    h_two = flat((normed_two * (1.0 + scale_two) + shift_two).astype(BF16))
    pre_act = jnp.dot(h_two, w_in, preferred_element_type=F32)
    activated, gelu_back = jax.vjp(partial(jax.nn.gelu, approximate=True), pre_act)
    act_low = activated.astype(BF16)
    mlp_out = jnp.dot(act_low, w_down, preferred_element_type=F32)
    block_output = (middle + gate_two * cube(mlp_out)).astype(BF16)

    grad_out = cot.astype(F32)
    d_mlp = flat((gate_two * grad_out).astype(BF16))
    g_down = jnp.dot(act_low.T, d_mlp, preferred_element_type=F32).astype(BF16)
    d_act = jnp.dot(d_mlp, w_down.T, preferred_element_type=F32)
    d_pre = gelu_back(d_act)[0].astype(BF16)
    g_in = jnp.dot(h_two.T, d_pre, preferred_element_type=F32).astype(BF16)
    d_htwo = cube(jnp.dot(d_pre, w_in.T, preferred_element_type=F32))
    d_gate_two = jnp.sum(grad_out * cube(mlp_out), axis=1)
    d_scale_two = jnp.sum(d_htwo * normed_two, axis=1)
    d_shift_two = jnp.sum(d_htwo, axis=1)
    d_middle = grad_out + norm_back(d_htwo * (1.0 + scale_two), normed_two, inv_two)
    d_attn = flat((gate_one * d_middle).astype(BF16))
    d_gate_one = jnp.sum(d_middle * cube(attn_out), axis=1)
    g_out = jnp.dot(attended.T, d_attn, preferred_element_type=F32).astype(BF16)
    d_attended = jnp.dot(d_attn, w_out.T, preferred_element_type=F32).astype(BF16)
    dq, dk, dv = attend_back(ends, queries, kv_all, d_attended, piece, per)
    dkv = jnp.concatenate([dk, dv], axis=1).reshape(per, rows, 2 * width)
    dkv_own = lax.dynamic_index_in_dim(dkv, g, 0, keepdims=False).astype(F32)
    for k in range(1, per):
        sent = lax.dynamic_index_in_dim(dkv, (g + k) % per, 0, keepdims=False)
        dkv_own = dkv_own + lax.ppermute(sent, "frame", partners(k)).astype(F32)
    d_proj = jnp.concatenate([dq * jnp.asarray(q_scale, BF16), dkv_own.astype(BF16)], axis=1)
    g_qkv = jnp.dot(h_one.T, d_proj, preferred_element_type=F32).astype(BF16)
    d_hone = cube(jnp.dot(d_proj, w_qkv.T, preferred_element_type=F32))
    d_scale_one = jnp.sum(d_hone * normed_one, axis=1)
    d_shift_one = jnp.sum(d_hone, axis=1)
    d_input = d_middle + norm_back(d_hone * (1.0 + scale_one), normed_one, inv_one)
    input_grad = d_input.astype(BF16)
    piece_dmod = jnp.stack([d_shift_one, d_scale_one, d_gate_one, d_shift_two, d_scale_two, d_gate_two])
    frame_dmod = jnp.einsum("pf,jpd->jfd", selector, piece_dmod, precision=HIGHEST)

    if direct:
        held_grad, dmod_parts = reduce_matrices(
            [g_qkv, g_out, g_in, g_down], frame_dmod.reshape(24, width), total, batch_size
        )
        dmod_all = jnp.sum(dmod_parts.reshape(4, 2, 4, 24, 128), axis=1).transpose(1, 0, 2, 3).reshape(384, 128)
        ada_grad = lax.dot_general(
            cond_all.astype(F32), dmod_all, (((0,), (0,)), ((), ())), precision=HIGHEST
        ).astype(BF16)
        edge = jnp.concatenate([ada_grad[FIRST * GROUP : FIRST * GROUP + 96], held_grad[96:GROUP]], axis=0)
        ordered_grad = jnp.concatenate([ada_grad[: FIRST * GROUP], edge, held_grad[GROUP:]], axis=0)
        cut_grad = pick_blocks(owned_block, ordered_grad.reshape(total, GROUP, 128))
        grad_block, outputs, input_grads = collect_blocks(cut_grad, block_output, input_grad, total, batch_size)
        shard_total = lax.dot_general(
            swap, grad_block, (((0,), (0,)), ((), ())), preferred_element_type=F32
        ).reshape(1, block_size)
    else:
        outputs, input_grads = swap_videos([block_output, input_grad], videos, per, 1)
        g_ada = lax.dot_general(
            cond.astype(F32),
            frame_dmod.transpose(1, 0, 2).reshape(frame_count, 6 * width),
            (((0,), (0,)), ((), ())),
            precision=HIGHEST,
        )
        flat_grads = jnp.concatenate(
            [piece_grad.astype(F32).reshape(-1) for piece_grad in (g_ada, g_qkv, g_out, g_in, g_down)]
        )
        arranged = jnp.take(flat_grads.reshape(-1, block_size), owned_block, axis=0).reshape(-1)
        shard_total = lax.psum_scatter(
            arranged, ("frame", "batch"), scatter_dimension=0, tiled=True
        ).reshape(1, block_size)
    new_first = BETA_ONE * first_moment + (1.0 - BETA_ONE) * shard_total
    new_second = BETA_TWO * second_moment + (1.0 - BETA_TWO) * shard_total * shard_total
    fix_one = 1.0 - BETA_ONE**STEP
    fix_two = 1.0 - BETA_TWO**STEP
    update = new_first / fix_one / (jnp.sqrt(new_second / fix_two) + ADAM_EPS)
    new_master = master - LEARN_RATE * (update + WEIGHT_DECAY * master)
    return (outputs, input_grads, new_master, new_first, new_second)


def solution(mesh):
    placed = (
        P("batch", "frame", None),
        P("batch", "frame", None),
        P("batch"),
        P("batch", None),
        P(),
        P(("frame", "batch"), None),
        P(("frame", "batch"), None),
        P(("frame", "batch"), None),
    )
    return jax.shard_map(
        partial(shards, mesh.shape["frame"], mesh.shape["batch"]),
        mesh=mesh,
        in_specs=placed,
        out_specs=(
            P("batch", "frame", None),
            P("batch", "frame", None),
            P(("frame", "batch"), None),
            P(("frame", "batch"), None),
            P(("frame", "batch"), None),
        ),
        check_vma=False,
    )
```

time: 2940 us -> 665 us (0.23)
  waiting for transfers between devices: 1530 us -> 0.01 us
  local copies, waits for them, and re-layouts: 1000 us -> 28.3 us
  Pallas kernels: 0 us -> 458 us
  matrix products: 234 us -> 98.6 us
  other arithmetic: 148 us -> 66.2 us
    unnamed x19 -> x0, waiting for transfers between devices: 1140 us -> none
    gather x18 -> x0, local copies, waits for them, and re-layouts: 468 us -> none  [the longest x11 308 us: shards(): placed = jnp.take(gathered, jnp.argsort(owned_block), axis=0).reshape(-1)]
    pallas_call x0 -> x8, Pallas kernels: none -> 458 us  [the longest x1 153 us: gather_matrices(): pl.pallas_call(partial(gather_kernel, total, batch), out_shape=[jax.Shape...]
    all_gather x9 -> x0, waiting for transfers between devices: 392 us -> none  [the longest x1 392 us: shards(): lax.all_gather(master.astype(jnp.bfloat16), ('frame', 'batch'), axis=0, t...]
    unnamed x259 -> x60, local copies, waits for them, and re-layouts: 347 us -> 7.66 us
    dot_general x72 -> x19, matrix products: 234 us -> 98.6 us  [the longest x1 15.8 us: shards(): pre_act = jnp.dot(h_two, w_in, preferred_element_type=F32)]
    reshape x1 -> x2, local copies, waits for them, and re-layouts: 64.3 us -> 0.7 us  [the longest x1 0.68 us: shards(): frame_dmod.reshape(24, width)]
    another operation x13 -> x2, local copies, waits for them, and re-layouts: 62.9 us -> 0.01 us  [the longest x1 0.01 us: shards(): jnp.stack([d_shift_one, d_scale_one, d_gate_one, d_shift_two, d_scale_two...]
  transfers between devices with their start and end apart: 14 -> 2, of which waited for: 4 -> 0; matrix products, arithmetic and copies ran while one was open for 14% -> 4% of each run, Pallas kernels for 0% -> 0%
where the time goes in v1:
time: 665 us; the launch traced here: 656 us
  Pallas kernels  458 us (69%)
  matrix products  98.6 us (15%)
  other arithmetic  66.2 us (10%)
  local copies, waits for them, and re-layouts  28.3 us (4%)
    pallas_call x1, Pallas kernels, gather_matrices(): pl.pallas_call(partial(gather_kernel, total, batch), out_shape=[jax.Shape...  153 us
    pallas_call x1, Pallas kernels, reduce_matrices(): pl.pallas_call(partial(reduce_kernel, total, batch), out_shape=[jax.Shape...  148 us
    pallas_call x1, Pallas kernels, scatter_blocks(): pl.pallas_call(partial(scatter_kernel, total, batch), out_shape=[jax.Shap...  45.3 us
    pallas_call x1, Pallas kernels, collect_blocks(): pl.pallas_call(partial(collect_kernel, total, batch), out_shape=[jax.Shap...  44.7 us
    pallas_call x1, Pallas kernels, attend_back(): pl.pallas_call(partial(attend_back_kernel, piece, per), grid_spec=pltpu.P...  37.8 us
    convert_element_type x1, other arithmetic, shards(): master.reshape(ROWS, 1024).astype(BF16)  25.5 us
    pallas_call x1, Pallas kernels, attend(): pl.pallas_call(partial(attend_kernel, piece, per), grid_spec=pltpu.Prefet...  22.9 us
    sub x1, other arithmetic, shards(): new_master = master - LEARN_RATE * (update + WEIGHT_DECAY * master)  18.3 us
  transfers between devices with their start and end apart: 2, of which 0 were waited for; matrix products, arithmetic and copies ran while one was open for 4% of the time, Pallas kernels for 0%

profile of v1, /device:TPU:0, one launch (start us, length us, event | category | flops | bytes accessed | tf_op | source)
XLA Modules:
  0.0 656.0 jit_solution(3303455134481728014)
XLA Ops:
  6.8 25.5 %convert_reduce_fusion.1 = bf16[589824]{0:T(1024)(128)(2,1)S(1)} fusion(f32[1,589824]{1,0:T(1,128)} %param.16), kind=kLoop, calls=%fused_computation.37 | loop fusion | flops 589824 | bytes 3538944 | tf_op jit(solution)/shard_map/convert_element_type | solution.py:839
  36.4 45.3 %scatter_blocks.1 = (bf16[32,144,128]{2,1,0:T(8,128)(2,1)}, s32[4,8,128]{2,1,0:T(8,128)}, bf16[4,128,1024]{2,1,0:T(8,128)(2,1)}, bf16[4,128,1024]{2,1,0:T(8,128)(2,1)}) custom-call(bf16[576,1024]{1,0:T(8,128)(2,1)} %convolution_convert_fusion.4.blk, s32[8,128]{1,0:T(8,128)} %scatter.4.levels, bf16[4,128,1024]{2,1,0:T(8,128)(2,1)} %tok.1, ...), custom_call_target="tpu_custom_call" | custom-call | tf_op jit(solution)/shard_map/scatter_blocks/pallas_call | solution.py:204
  81.7 2.6 pick_blocks.2
  96.0 153.5 %gather_matrices.1 = (bf16[1024,3072]{1,0:T(8,128)(2,1)}, bf16[1024,1024]{1,0:T(8,128)(2,1)}, bf16[1024,4096]{1,0:T(8,128)(2,1)}, bf16[4096,1024]{1,0:T(8,128)(2,1)}, f32[4,24,1024]{2,1,0:T(8,128)}) custom-call(bf16[3168,128]{1,0:T(8,128)(2,1)} %bitcast.131, f32[16,24,128]{2,1,0:T(8,128)} %fusion.55.mod), custom_call_target="tpu_custom_call" | custom-call | tf_op jit(solution)/shard_map/gather_matrices/pallas_call | solution.py:413
  252.6 5.5 fusion.56
  258.1 2.9 broadcast_in_dim.10
  261.0 2.6 bitcast_dynamic-update-slice_fusion.1
  265.8 3.2 fusion.29.q
  269.0 10.1 %fusion.58 = f32[512,4096]{1,0:T(8,128)} fusion(bf16[512,1024]{1,0:T(8,128)(2,1)S(1)} %bitcast.136, bf16[4096,1024]{1,0:T(8,128)(2,1)} %get-tuple-element.43), kind=kOutput, calls=%fused_computation.150 | convolution fusion | flops 4294967296 | bytes 17825792 | tf_op jit(solution)/shard_map/dot_general | solution.py:908
  279.1 3.1 bitcast_dynamic-update-slice_fusion
  282.2 22.9 %attend.1 = bf16[512,1024]{1,0:T(8,128)(2,1)} custom-call(s32[4]{0:T(128)} %get-tuple-element.68.ends, bf16[512,1024]{1,0:T(8,128)(2,1)} %fusion.29.q, bf16[1024,2048]{1,0:T(8,128)(2,1)} %bitcast.13.k.v, bf16[1024,2048]{1,0:T(8,128)(2,1)} %bitcast.13.k.v), custom_call_target="tpu_custom_call" | custom-call | flops 2147483648 | bytes 6291456 | tf_op jit(solution)/shard_map/attend/pallas_call | solution.py:697
  309.0 15.8 %fusion.6 = (bf16[512,4096]{1,0:T(8,128)(2,1)S(1)}, f32[512,4096]{1,0:T(8,128)}) fusion(f32[512,4096]{1,0:T(8,128)} %fusion.58, bf16[512,1024]{1,0:T(8,128)(2,1)S(1)} %bitcast.138, bf16[1024,4096]{1,0:T(8,128)(2,1)} %get-tuple-element.44), kind=kOutput, calls=%fused_computation.8 | convolution fusion | flops 4336910336 | bytes 30408704 | tf_op jit(solution)/shard_map/dot_general | solution.py:899
  324.8 8.6 %fusion.31 = (f32[512]{0:T(512)S(1)}, f32[512,1024]{1,0:T(8,128)S(1)}) fusion(f32[4,1024]{1,0:T(4,128)S(1)} %get-tuple-element.76, bf16[512,4096]{1,0:T(8,128)(2,1)S(1)} %get-tuple-element.82, bf16[1024,4096]{1,0:T(8,128)(2,1)} %get-tuple-element.44), kind=kOutput, calls=%fused_computation.57 | convolution fusion | flops 4296015360 | bytes 14698496 | tf_op jit(solution)/shard_map/dot_general | solution.py:911
  334.7 9.6 %add_convert_fusion = (bf16[4,128,1024]{2,1,0:T(8,128)(2,1)}, f32[4,1024]{1,0:T(4,128)S(1)}, f32[4,1024]{1,0:T(4,128)S(1)}, f32[4,128,1024]{2,1,0:T(8,128)S(1)}) fusion(f32[4,128,1024]{2,1,0:T(8,128)S(1)} %get-tuple-element.65, f32[4,1024]{1,0:T(4,128)S(1)} %get-tuple-element.74, bf16[4,128,1024]{2,1,0:T(8,128)(2,1)S(1)} %copy-done.4, ...), kind=kOutput, calls=%fused_computation.63 | convolution fusion | flops 4322222080 | bytes 27336704 | tf_op jit(solution)/shard_map/dot_general | solution.py:902
  350.9 6.7 %convolution_convert_fusion.1.refs_2_ = bf16[1024,4096]{1,0:T(8,128)(2,1)} fusion(bf16[512,1024]{1,0:T(8,128)(2,1)S(1)} %bitcast.139, bf16[512,4096]{1,0:T(8,128)(2,1)S(1)} %copy-done.20), kind=kOutput, calls=%fused_computation.11 | convolution fusion | flops 4299161600 | bytes 13631488 | tf_op jit(solution)/shard_map/dot_general | solution.py:910
  357.6 37.8 %attend_back.1 = (bf16[512,1024]{1,0:T(8,128)(2,1)}, bf16[1024,1024]{1,0:T(8,128)(2,1)}, bf16[1024,1024]{1,0:T(8,128)(2,1)}) custom-call(s32[4]{0:T(128)} %get-tuple-element.68.ends, bf16[512,1024]{1,0:T(8,128)(2,1)} %fusion.29.q, bf16[1024,2048]{1,0:T(8,128)(2,1)} %bitcast.13.k.v, bf16[1024,2048]{1,0:T(8,128)(2,1)} %bitcast.13.k.v, ...), custom_call_target="tpu_custom_call" | custom-call | flops 5368709120 | bytes 9437184 | tf_op jit(solution)/shard_map/attend_back/pallas_call | solution.py:745
  399.8 13.3 %convolution_convert_fusion.refs_3_ = bf16[4096,1024]{1,0:T(8,128)(2,1)} fusion(bf16[512,1024]{1,0:T(8,128)(2,1)} %bitcast.137, f32[512,4096]{1,0:T(8,128)} %get-tuple-element.83), kind=kOutput, calls=%fused_computation.10 | convolution fusion | flops 4318035968 | bytes 17825792 | tf_op jit(solution)/shard_map/dot_general | solution.py:907
  414.0 3.5 bitcast_multiply_fusion.1
  417.5 5.9 convolution_convert_fusion.2.refs_0_
  425.4 148.4 %reduce_matrices.1 = (bf16[3168,128]{1,0:T(8,128)(2,1)}, f32[32,24,128]{2,1,0:T(8,128)}) custom-call(bf16[1024,3072]{1,0:T(8,128)(2,1)} %convolution_convert_fusion.2.refs_0_, bf16[1024,1024]{1,0:T(8,128)(2,1)} %convolution_convert_fusion.3.refs_1_, bf16[1024,4096]{1,0:T(8,128)(2,1)} %convolution_convert_fusion.1.refs_2_, ...), custom_call_target="tpu_custom_call" | custom-call | tf_op jit(solution)/shard_map/reduce_matrices/pallas_call | solution.py:616
  574.9 2.8 fusion.59
  581.5 3.2 fusion.25.grad
  584.7 44.7 %collect_blocks.1 = (bf16[576,1024]{1,0:T(8,128)(2,1)}, bf16[4,128,1024]{2,1,0:T(8,128)(2,1)}, bf16[4,128,1024]{2,1,0:T(8,128)(2,1)}) custom-call(bf16[32,144,128]{2,1,0:T(8,128)(2,1)} %pick_blocks.3.cut, bf16[4,128,1024]{2,1,0:T(8,128)(2,1)} %get-tuple-element.70.act, bf16[4,128,1024]{2,1,0:T(8,128)(2,1)} %fusion.25.grad), custom_call_target="tpu_custom_call" | custom-call | tf_op jit(solution)/shard_map/collect_blocks/pallas_call | solution.py:265
  634.6 18.3 %multiply_subtract_fusion = (f32[1,589824]{1,0:T(1,128)}, f32[1,589824]{1,0:T(1,128)}, f32[1,589824]{1,0:T(1,128)}) fusion(f32[1,589824]{1,0:T(1,128)S(1)} %copy-done.2, f32[1,589824]{1,0:T(1,128)S(1)} %bitcast.123, f32[1,589824]{1,0:T(1,128)S(1)} %copy-done.6, f32[1,589824]{1,0:T(1,128)S(1)} %copy-done.7), kind=kLoop, calls=%fused_computation.36 | loop fusion | flops 8257536 | bytes 16515072 | tf_op jit(solution)/shard_map/sub | solution.py:971
  (138 shorter events, 55.5 us)
Async XLA Ops:
  81.7 4.8 copy-start.18
  81.7 6.8 %copy-start.15 = (s32[4,8,128]{2,1,0:T(8,128)S(1)}, s32[4,8,128]{2,1,0:T(8,128)}, u32[]{:S(2)}) copy-start(s32[4,8,128]{2,1,0:T(8,128)} %get-tuple-element.35) | copy-start | bytes 49156
  81.7 6.9 %copy-start = (bf16[4,128,1024]{2,1,0:T(8,128)(2,1)S(1)}, bf16[4,128,1024]{2,1,0:T(8,128)(2,1)}, u32[]{:S(2)}) copy-start(bf16[4,128,1024]{2,1,0:T(8,128)(2,1)} %get-tuple-element.36) | copy-start | bytes 3145732
  91.4 2.0 slice-start.4
  258.1 5.5 copy-start.5
  263.6 1.9 copy-start.3
  263.6 15.4 %collective-permute-start = (bf16[512,2048]{1,0:T(8,128)(2,1)}, bf16[512,2048]{1,0:T(8,128)(2,1)}, u32[]{:S(2)}, u32[]{:S(2)}) collective-permute-start(bf16[512,2048]{1,0:T(8,128)(2,1)} %get-tuple-element.67), channel_id=1, source_target_pairs={{0,4},{4,0},{8,12},{12,8},{16,20},{20,16},{24,28},{28,24},{1,5},{5... | collective-permute-start | bytes 6291464 | tf_op jit(solution)/shard_map/ppermute | solution.py:891
  265.8 13.3 %copy-start.10 = (bf16[4,128,1024]{2,1,0:T(8,128)(2,1)}, bf16[4,128,1024]{2,1,0:T(8,128)(2,1)S(1)}, u32[]{:S(2)}) copy-start(bf16[4,128,1024]{2,1,0:T(8,128)(2,1)S(1)} %fusion.27) | copy-start | bytes 3145732
  282.2 22.9 %copy-start.16 = (bf16[1024,1024]{1,0:T(8,128)(2,1)S(1)}, bf16[1024,1024]{1,0:T(8,128)(2,1)}, u32[]{:S(2)}) copy-start(bf16[1024,1024]{1,0:T(8,128)(2,1)} %get-tuple-element.42) | copy-start | bytes 6291460
  308.3 26.2 %slice-start = ((s8[8388608]{0:T(1024)(128)(4,1)}), s8[4194304]{0:T(1024)(128)(4,1)S(1)}, s32[]{:S(2)}) async-start(s8[8388608]{0:T(1024)(128)(4,1)} %bitcast.125), calls=%async_computation | async-start | bytes 8388608
  309.0 25.5 %slice-start.1 = ((s8[8388608]{0:T(1024)(128)(4,1)}), s8[4194304]{0:T(1024)(128)(4,1)S(1)}, s32[]{:S(2)}) async-start(s8[8388608]{0:T(1024)(128)(4,1)} %bitcast.125), calls=%async_computation.1 | async-start | bytes 8388608
  324.8 8.6 %copy-start.19 = (bf16[512,4096]{1,0:T(8,128)(2,1)}, bf16[512,4096]{1,0:T(8,128)(2,1)S(1)}, u32[]{:S(2)}) copy-start(bf16[512,4096]{1,0:T(8,128)(2,1)S(1)} %get-tuple-element.82) | copy-start | bytes 12582916
  346.0 2.3 copy-start.21
  348.3 2.6 copy-start.20
  398.0 15.9 %slice-start.2 = ((s8[6291456]{0:T(1024)(128)(4,1)}), s8[4194304]{0:T(1024)(128)(4,1)S(1)}, s32[]{:S(2)}) async-start(s8[6291456]{0:T(1024)(128)(4,1)} %bitcast.127), calls=%async_computation.2 | async-start | bytes 8388608
  399.5 13.7 %collective-permute-start.1 = (bf16[512,2048]{1,0:T(8,128)(2,1)}, bf16[512,2048]{1,0:T(8,128)(2,1)S(1)}, u32[]{:S(2)}, u32[]{:S(2)}) collective-permute-start(bf16[512,2048]{1,0:T(8,128)(2,1)} %dynamic-slice_bitcast_fusion), channel_id=1, source_target_pairs={{0,4},{4,0},{8,12},{12,8},{16,20},{20,16},{24,28},{28,24},{1,5},{5... | collective-permute-start | bytes 6291464 | tf_op jit(solution)/shard_map/ppermute | solution.py:925
  399.8 14.2 %slice-start.3 = ((s8[6291456]{0:T(1024)(128)(4,1)}), s8[2097152]{0:T(1024)(128)(4,1)S(1)}, s32[]{:S(2)}) async-start(s8[6291456]{0:T(1024)(128)(4,1)} %bitcast.127), calls=%async_computation.3 | async-start | bytes 4194304
  414.0 3.5 copy-start.9
  417.5 6.1 copy-start.1
  574.9 2.9 copy-start.14
  629.5 5.1 copy-start.7
  632.1 2.5 copy-start.2
  632.1 2.5 copy-start.6
  634.6 18.3 %copy-start.12 = (bf16[4,128,1024]{2,1,0:T(8,128)(2,1)S(1)}, bf16[4,128,1024]{2,1,0:T(8,128)(2,1)}, u32[]{:S(2)}) copy-start(bf16[4,128,1024]{2,1,0:T(8,128)(2,1)} %get-tuple-element.105) | copy-start | bytes 3145732
  (5 other events, 7.1 us)

commit v2 on v1

--- a/solution.py
+++ b/solution.py
@@ -296,9 +296,61 @@
     return pl.ds(pl.multiple_of(first, 128), count)
 
 
-def gather_kernel(total, batch, held, mod, *refs):
-    mats = dict(zip([kind for kind, _, _ in KINDS], refs[:4]))
-    mod_out, zsend, zrecv, psend, precv, msend, mrecv, own = refs[4:]
+UNITS = (
+    [("qkv", 0, 1024, 1024 * j) for j in range(3)]
+    + [("out", 0, 1024, 0)]
+    + [("in", 0, 1024, 1024 * j) for j in range(4)]
+    + [("down", 0, 1216, 0), ("down", 1216, 1152, 0), ("down", 2368, 1152, 0), ("down", 3520, 576, 0)]
+)
+DOWN_READY = (1152, 2304, 3456, 4096)
+DEALS = (
+    [("qkv", j, 0, 1024) for j in range(3)]
+    + [("out", 0, 0, 1024), ("in", None, 0, 1024)]
+    + [("down", 0, first, count) for first, count in ((0, 1216), (1216, 1152), (2368, 1152), (3520, 576))]
+)
+DEAL_OF = (0, 1, 2, 3, 4, 4, 4, 4, 5, 6, 7, 8)
+DEAL_ROWS = (256, 256, 256, 256, 1024, 304, 288, 288, 144)
+
+
+def deal_pieces(d, z):
+    kind, j, first, count = DEALS[d]
+    last = first + count
+    found = []
+    for row, rows, to, col in pieces(kind, z):
+        base = pieces(kind, 0)[len(found)][2] if kind == "down" else None
+        found.append((row, rows, to, col, base))
+    if kind == "down":
+        return [p[:4] for p in found if first <= p[4] < last]
+    if kind == "qkv":
+        return [p[:4] for p in found if p[3] == j]
+    return [p[:4] for p in found]
+
+
+GELU_A = math.sqrt(2.0 / math.pi)
+GELU_B = 0.044715
+
+
+def row_loop(count, step, body):
+    def one(i, carry):
+        body(pl.multiple_of(i * step, step))
+        return carry
+
+    lax.fori_loop(0, count // step, one, 0)
+
+
+def norm_rows(values):
+    centre = values - jnp.mean(values, axis=-1, keepdims=True)
+    inv_std = lax.rsqrt(jnp.mean(centre * centre, axis=-1, keepdims=True) + 1e-06)
+    return centre * inv_std, inv_std
+
+
+def forward_kernel(total, batch, piece, per, sel, ends, tok, held, mod, *refs):
+    hbm, vm, sems = refs[:17], refs[17:33], refs[33:]
+    wq_o, wo_o, wi_o, wd_o, h1_o, q_o, kv_o, att_o, a_o, x1_o, h2_o, gp_o, u_o, m_o, y_o, pm_o, mod_in = hbm
+    wq, wo, wi, wd, h1, q, kv, att, a, x1, h2, gp, u, m, pm, mod_v = vm
+    zsend, zrecv, psend, precv, msend, mrecv, own, wsem, osem, kvsend, kvrecv = sems
+    mats = {"qkv": wq, "out": wo, "in": wi, "down": wd}
+    mats_o = {"qkv": wq_o, "out": wo_o, "in": wi_o, "down": wd_o}
     y, x, c, z, at_x, at_y, at_c = plane()
     f = 4 * y + 2 * x + c
     me = f * batch + z
@@ -310,7 +362,7 @@
         of, oz = other // batch, other % batch
         copy = pltpu.make_async_remote_copy(
             src_ref=mod.at[4 * oz + of // 2],
-            dst_ref=mod_out.at[z, :, lanes(128 * strip, 128)],
+            dst_ref=mod_v.at[z, :, lanes(128 * strip, 128)],
             send_sem=msend.at[k],
             recv_sem=mrecv.at[k],
             device_id=(of, oz),
@@ -321,31 +373,34 @@
         else:
             copy.wait()
 
-    sends = []
-    for m, (kind, _, _) in enumerate(KINDS):
+    def spot(kind, to, count, j):
+        return mats[kind].at[pl.ds(pl.multiple_of(to, 16), count), lanes(1024 * j + 128 * strip, 128)]
+
+    for d, (kind, _, _, _) in enumerate(DEALS):
         for k in range(1, batch):
-            for row, count, to, j in pieces(kind, z):
-                src = held.at[pl.ds(row, count)]
-                dst = mats[kind].at[pl.ds(pl.multiple_of(to, 16), count), lanes(1024 * j + 128 * strip, 128)]
-                remote(src, dst, zsend.at[m, k], zrecv.at[m, k], (f, (z + k) % batch))
-        for row, count, to, j in pieces(kind, z):
-            local(
-                held.at[pl.ds(row, count)],
-                mats[kind].at[pl.ds(pl.multiple_of(to, 16), count), lanes(1024 * j + 128 * strip, 128)],
-                own.at[m],
-            )
-        if m == 0:
-            lax.fori_loop(1, total, lambda k, cc: (mod_group(k, True), cc)[1], 0)
-    mod_own = local(mod.at[4 * z + f // 2], mod_out.at[z, :, lanes(128 * strip, 128)], own.at[4])
-
-    def whole(m):
-        lo, hi = SPANS[KINDS[m][0]]
-        return held.at[pl.ds(lo, hi - lo)]
-
-    def z_wait(m):
+            for row, count, to, j in deal_pieces(d, z):
+                remote(
+                    held.at[pl.ds(row, count)], spot(kind, to, count, j), zsend.at[d, k], zrecv.at[d, k],
+                    (f, (z + k) % batch),
+                )
+        for row, count, to, j in deal_pieces(d, z):
+            local(held.at[pl.ds(row, count)], spot(kind, to, count, j), own.at[d])
+        if d == 0:
+            lax.fori_loop(1, total, lambda k, t: (mod_group(k, True), t)[1], 0)
+            mod_own = local(mod.at[4 * z + f // 2], mod_v.at[z, :, lanes(128 * strip, 128)], own.at[len(DEALS)])
+
+    def whole(d):
+        return held.at[pl.ds(0, DEAL_ROWS[d])]
+
+    dealt = set()
+
+    def deal_wait(d):
+        if d in dealt:
+            return
+        dealt.add(d)
         for k in range(1, batch):
-            pltpu.make_async_copy(whole(m), whole(m), zrecv.at[m, k]).wait()
-        pltpu.make_async_copy(whole(m), whole(m), own.at[m]).wait()
+            pltpu.make_async_copy(whole(d), whole(d), zrecv.at[d, k]).wait()
+        pltpu.make_async_copy(whole(d), whole(d), own.at[d]).wait()
 
     slots = {}
     counter = [0]
@@ -356,78 +411,263 @@
         ref = mat.at[pl.ds(row, count), lanes(col, width)]
         slots.setdefault(key, []).append(remote(ref, ref, psend.at[s], precv.at[s], device))
 
-    def first(m):
-        kind, depth, blocks = KINDS[m]
-        half = depth // 2
-        for j in range(blocks):
-            push((m, 1), mats[kind], 0, half, 1024 * j + 128 * strip, 128, at_x)
-            push((m, 1), mats[kind], half, half, 1024 * j + 128 * strip, 128, at_y)
-
-    def second(m):
-        kind, depth, blocks = KINDS[m]
-        half = depth // 2
-        for copy in slots[(m, 1)]:
+    def stage_a(n):
+        kind, row, rows, col = UNITS[n]
+        half = rows // 2
+        deal_wait(DEAL_OF[n])
+        push((n, 1), mats[kind], row, half, col + 128 * strip, 128, at_x)
+        push((n, 1), mats[kind], row + half, half, col + 128 * strip, 128, at_y)
+
+    def stage_b(n):
+        kind, row, rows, col = UNITS[n]
+        half = rows // 2
+        for copy in slots[(n, 1)]:
             copy.wait_recv()
-        for j in range(blocks):
-            push((m, 2), mats[kind], 0, half, 1024 * j + 512 * c + 256 * y, 256, at_y)
-            for yy in range(2):
-                push((m, 2), mats[kind], half, half, 1024 * j + 512 * c + 256 * yy + 128 * x, 128, at_x)
-
-    def third(m):
-        kind, depth, blocks = KINDS[m]
-        for copy in slots[(m, 2)]:
+        push((n, 2), mats[kind], row, half, col + 512 * c + 256 * y, 256, at_y)
+        for yy in range(2):
+            push((n, 2), mats[kind], row + half, half, col + 512 * c + 256 * yy + 128 * x, 128, at_x)
+
+    def stage_c(n):
+        kind, row, rows, col = UNITS[n]
+        for copy in slots[(n, 2)]:
             copy.wait_recv()
-        for j in range(blocks):
-            push((m, 3), mats[kind], 0, depth, 1024 * j + 512 * c, 512, at_c)
-
-    z_wait(0)
-    first(0)
-    z_wait(1)
-    first(1)
-    second(0)
-    z_wait(2)
-    first(2)
-    second(1)
-    third(0)
-    z_wait(3)
-    first(3)
-    second(2)
-    third(1)
-    second(3)
-    third(2)
-    third(3)
-    for m in range(4):
-        for copy in slots[(m, 3)]:
+        push((n, 3), mats[kind], row, rows, col + 512 * c, 512, at_c)
+
+    saves = []
+
+    def ready(n):
+        kind, row, rows, col = UNITS[n]
+        for copy in slots[(n, 3)]:
             copy.wait_recv()
+        ref = (pl.ds(row, rows), pl.ds(col, 1024))
+        saves.append(local(mats[kind].at[ref], mats_o[kind].at[ref], wsem.at[n]))
+
+    pumped = [0]
+    last_unit = len(UNITS)
+
+    def pump():
+        s = pumped[0]
+        pumped[0] += 1
+        if 0 <= s - 2 < last_unit:
+            stage_b(s - 2)
+        if s < last_unit:
+            stage_a(s)
+        if 0 <= s - 3 < last_unit:
+            stage_c(s - 3)
+
+    def pump_to(s):
+        while pumped[0] <= s:
+            pump()
+
+    def save(src, dst, n):
+        saves.append(local(src, dst, osem.at[n]))
+
+    pump_to(0)
+    lax.fori_loop(1, total, lambda k, t: (mod_group(k, False), t)[1], 0)
+    mod_own.wait()
+    for j in range(6):
+        for p in range(4):
+            value = jnp.zeros((1, 1024), F32)
+            for fr in range(4):
+                row = mod_v[0, pl.ds(4 * j + fr, 1), :]
+                for s in range(1, batch):
+                    row = row + mod_v[s, pl.ds(4 * j + fr, 1), :]
+                value = value + sel[p, fr] * row
+            pm[pl.ds(4 * j + p, 1), :] = value
+    save(pm, pm_o, 0)
+
+    def mod_row(j, p):
+        return pm[pl.ds(4 * j + p, 1), :]
+
+    step = 32
+    for p in range(4):
+        shift, scale = mod_row(0, p), mod_row(1, p)
+
+        def one(i, p=p, shift=shift, scale=scale):
+            rows = pl.ds(pl.multiple_of(p * piece + i, step), step)
+            normed, _ = norm_rows(tok[rows, :].astype(F32))
+            h1[rows, :] = (normed * (1.0 + scale) + shift).astype(BF16)
+
+        row_loop(piece, step, one)
+    save(h1, h1_o, 1)
+
+    pump_to(4)
+    for j in range(3):
+        pump_to(3 + j)
+        ready(j)
+
+        def cols(n, j=j):
+            value = jnp.dot(h1[...], wq[:, lanes(1024 * j + n, 512)], preferred_element_type=F32)
+            if j == 0:
+                q[:, lanes(n, 512)] = (value * HD ** (-0.5)).astype(BF16)
+            else:
+                kv[c, :, lanes(1024 * (j - 1) + n, 512)] = value.astype(BF16)
+
+        row_loop(1024, 512, cols)
+    save(q, q_o, 2)
+    kv_copy = remote(kv.at[c], kv.at[c], kvsend, kvrecv, at_c)
+    pump_to(6)
+    kv_copy.wait_recv()
+    save(kv, kv_o, 3)
+
+    keys = 2 * 4 * piece
+    end_of = [ends[t] for t in range(4)]
+
+    def heads(h):
+        outs = []
+        for e in range(2):
+            def part(ref_cols):
+                return lanes(ref_cols, 128)
+
+            k_pair = kv[:, :, part(128 * h)].reshape(keys, 128)
+            v_pair = kv[:, :, part(1024 + 128 * h)].reshape(keys, 128)
+            q_pair = q[:, part(128 * h)]
+            cut = slice(64 * e, 64 * e + 64)
+            s = scores_t(k_pair[:, cut], q_pair[:, cut], end_of, piece, per)
+            peak = jnp.max(s, axis=0, keepdims=True)
+            w = jnp.exp(s - peak)
+            prob = (w * (1.0 / jnp.sum(w, axis=0, keepdims=True))).astype(BF16)
+            outs.append(
+                lax.dot_general(prob, v_pair[:, cut], (((0,), (0,)), ((), ())), preferred_element_type=F32)
+            )
+        att[:, lanes(128 * h, 128)] = jnp.concatenate(outs, axis=1).astype(BF16)
+
+    for n in range(4):
+        lax.fori_loop(2 * n, 2 * n + 2, lambda h, t: (heads(h), t)[1], 0)
+        pump_to(7 + n)
+    save(att, att_o, 4)
+
+    ready(3)
+
+    def out_cols(n):
+        a[:, lanes(n, 512)] = jnp.dot(att[...], wo[:, lanes(n, 512)], preferred_element_type=F32)
+
+    row_loop(1024, 512, out_cols)
+    save(a, a_o, 5)
+    for p in range(4):
+        gate, shift, scale = mod_row(2, p), mod_row(3, p), mod_row(4, p)
+
+        def two(i, p=p, gate=gate, shift=shift, scale=scale):
+            rows = pl.ds(pl.multiple_of(p * piece + i, step), step)
+            middle = tok[rows, :].astype(F32) + gate * a[rows, :]
+            x1[rows, :] = middle
+            normed, _ = norm_rows(middle)
+            h2[rows, :] = (normed * (1.0 + scale) + shift).astype(BF16)
+
+        row_loop(piece, step, two)
+    save(x1, x1_o, 6)
+    save(h2, h2_o, 7)
+
+    for j in range(4):
+        pump_to(11 + j)
+        ready(4 + j)
+
+        def in_cols(n, j=j):
+            col = 1024 * j + n
+            pre = jnp.dot(h2[...], wi[:, lanes(col, 256)], preferred_element_type=F32)
+            square = pre * pre
+            t = jnp.tanh(GELU_A * (pre + GELU_B * (square * pre)))
+            lift = 0.5 * (1.0 + t)
+            u[:, lanes(col, 256)] = (pre * lift).astype(BF16)
+            slope = lift + (0.5 * GELU_A) * pre * (1.0 - t * t) * (1.0 + 3.0 * GELU_B * square)
+            gp[:, lanes(col, 256)] = slope.astype(BF16)
+
+        row_loop(1024, 256, in_cols)
+    save(u, u_o, 8)
+    save(gp, gp_o, 9)
+    before = 0
+    for n in range(4):
+        ready(8 + n)
+        depth = DOWN_READY[n] - before
+
+        def down_cols(col, n=n, before=before, depth=depth):
+            part = jnp.dot(
+                u[:, pl.ds(before, depth)], wd[pl.ds(before, depth), lanes(col, 512)], preferred_element_type=F32
+            )
+            if n == 0:
+                m[:, lanes(col, 512)] = part
+            else:
+                m[:, lanes(col, 512)] = m[:, lanes(col, 512)] + part
+
+        row_loop(1024, 512, down_cols)
+        before = DOWN_READY[n]
+    save(m, m_o, 10)
+    for p in range(4):
+        gate = mod_row(5, p)
+
+        def three(i, p=p, gate=gate):
+            rows = pl.ds(pl.multiple_of(p * piece + i, step), step)
+            h1[rows, :] = (x1[rows, :] + gate * m[rows, :]).astype(BF16)
+
+        if p == 0:
+            saves[1].wait()
+        row_loop(piece, step, three)
+    saves_h1 = saves[1]
+    save(h1, y_o, 11)
+    for copy in saves:
+        if copy is not saves_h1:
+            copy.wait()
+    kv_copy.wait_send()
     for copies in slots.values():
         for copy in copies:
             copy.wait_send()
-    for m in range(4):
+    for d in range(len(DEALS)):
         for k in range(1, batch):
-            pltpu.make_async_copy(whole(m), whole(m), zsend.at[m, k]).wait()
-    mod_own.wait()
-    lax.fori_loop(1, total, lambda k, cc: (mod_group(k, False), cc)[1], 0)
-
-
-def gather_matrices(held, mod, total, batch):
+            pltpu.make_async_copy(whole(d), whole(d), zsend.at[d, k]).wait()
+
+
+def forward(sel, ends, tok, held, mod, total, batch, piece, per):
+    def out(*shape, dtype=BF16):
+        return jax.ShapeDtypeStruct(shape, dtype)
+
+    outs = [out(depth, 1024 * blocks) for _, depth, blocks in KINDS] + [
+        out(512, 1024),
+        out(512, 1024),
+        out(2, 512, 2048),
+        out(512, 1024),
+        out(512, 1024, dtype=F32),
+        out(512, 1024, dtype=F32),
+        out(512, 1024),
+        out(512, 4096),
+        out(512, 4096),
+        out(512, 1024, dtype=F32),
+        out(512, 1024),
+        out(24, 1024, dtype=F32),
+    ]
+    bufs = [pltpu.VMEM(o.shape, o.dtype) for o in outs[:14]] + [
+        pltpu.VMEM((24, 1024), F32),
+        pltpu.VMEM((batch, 24, 1024), F32),
+    ]
+    smem = pl.BlockSpec(memory_space=pltpu.SMEM)
+    dma = pltpu.SemaphoreType.DMA
     return pl.pallas_call(
-        partial(gather_kernel, total, batch),
-        out_shape=[jax.ShapeDtypeStruct((depth, 1024 * blocks), BF16) for _, depth, blocks in KINDS]
-        + [jax.ShapeDtypeStruct((batch, mod.shape[1], 1024), F32)],
-        in_specs=[ANY] * 2,
-        out_specs=[ANY] * 5,
-        scratch_shapes=[
-            pltpu.SemaphoreType.DMA((4, batch)),
-            pltpu.SemaphoreType.DMA((4, batch)),
-            pltpu.SemaphoreType.DMA((54,)),
-            pltpu.SemaphoreType.DMA((54,)),
-            pltpu.SemaphoreType.DMA((total,)),
-            pltpu.SemaphoreType.DMA((total,)),
-            pltpu.SemaphoreType.DMA((5,)),
+        partial(forward_kernel_entry, total, batch, piece, per),
+        out_shape=outs,
+        in_specs=[smem, smem, pl.BlockSpec(memory_space=pltpu.VMEM), ANY, ANY],
+        out_specs=[ANY] * len(outs),
+        scratch_shapes=bufs
+        + [
+            dma((len(DEALS), batch)),
+            dma((len(DEALS), batch)),
+            dma((6 * len(UNITS),)),
+            dma((6 * len(UNITS),)),
+            dma((total,)),
+            dma((total,)),
+            dma((len(DEALS) + 1,)),
+            dma((len(UNITS),)),
+            dma((12,)),
+            dma,
+            dma,
         ],
-        compiler_params=pltpu.CompilerParams(collective_id=1, has_side_effects=True),
-        name="gather_matrices",
-    )(held, mod)
+        compiler_params=pltpu.CompilerParams(
+            collective_id=1, has_side_effects=True, vmem_limit_bytes=VMEM_LIMIT
+        ),
+        name="forward",
+    )(sel, ends, tok, held, mod)
+
+
+def forward_kernel_entry(total, batch, piece, per, sel, ends, tok, held, mod, *refs):
+    forward_kernel(total, batch, piece, per, sel, ends, tok, held, mod, *refs[:16], None, *refs[16:])
 
 
 def add_rows(dst, dst_col, src, src_col, width, first, count):
@@ -662,6 +902,64 @@
     )(index, src)
 
 
+def cut_kernel(rows, master, out):
+    swap = (rows[...] == lax.broadcasted_iota(jnp.int32, (ROWS, ROWS), 1)).astype(BF16)
+    for s in range(8):
+        strip = master[pl.ds(s, ROWS, stride=8), :].astype(BF16)
+        out[:, 128 * s : 128 * s + 128] = jnp.dot(swap, strip, preferred_element_type=F32).astype(BF16)
+
+
+def cut_owned(rows, master):
+    whole = pl.BlockSpec(memory_space=pltpu.VMEM)
+    return pl.pallas_call(
+        cut_kernel,
+        out_shape=jax.ShapeDtypeStruct((ROWS, 1024), BF16),
+        in_specs=[whole, whole],
+        out_specs=whole,
+        compiler_params=pltpu.CompilerParams(vmem_limit_bytes=VMEM_LIMIT),
+        name="cut_owned",
+    )(rows, master)
+
+
+def adam(grad, master, first, second):
+    new_first = BETA_ONE * first + (1.0 - BETA_ONE) * grad
+    new_second = BETA_TWO * second + (1.0 - BETA_TWO) * grad * grad
+    fix_one = 1.0 - BETA_ONE**STEP
+    fix_two = 1.0 - BETA_TWO**STEP
+    update = new_first / fix_one / (jnp.sqrt(new_second / fix_two) + ADAM_EPS)
+    return master - LEARN_RATE * (update + WEIGHT_DECAY * master), new_first, new_second
+
+
+def update_kernel(rows, grad, master, first, second, new_master, new_first, new_second):
+    base = pl.program_id(0) * GROUP
+    swap = (rows[...] == base + lax.broadcasted_iota(jnp.int32, (GROUP, ROWS), 0)).astype(BF16)
+    for s in range(8):
+        at = pl.ds(s, GROUP, stride=8)
+        value = jnp.dot(swap, grad[:, 128 * s : 128 * s + 128], preferred_element_type=F32)
+        new_master[at, :], new_first[at, :], new_second[at, :] = adam(
+            value, master[at, :], first[at, :], second[at, :]
+        )
+
+
+def update_owned(rows, grad, master, first, second):
+    part = pl.BlockSpec((8 * GROUP, 128), lambda i: (i, 0))
+    return pl.pallas_call(
+        update_kernel,
+        grid=(ROWS // GROUP,),
+        out_shape=[jax.ShapeDtypeStruct(master.shape, F32)] * 3,
+        in_specs=[
+            pl.BlockSpec((1, ROWS), lambda i: (0, 0)),
+            pl.BlockSpec((ROWS, 1024), lambda i: (0, 0)),
+            part,
+            part,
+            part,
+        ],
+        out_specs=[part] * 3,
+        compiler_params=pltpu.CompilerParams(vmem_limit_bytes=VMEM_LIMIT),
+        name="update_owned",
+    )(rows, grad, master, first, second)
+
+
 def key_positions(rows, piece, per):
     i = lax.broadcasted_iota(jnp.int32, (rows, 1), 0)
     local_rows = rows // per
@@ -835,8 +1133,7 @@
         inverse = jnp.argsort(owned_block).astype(jnp.int32)
         table = jnp.asarray(np.stack([block_rows(b) for b in range(total)]).astype(np.int32))
         own_rows = lax.dynamic_index_in_dim(table, owned_block[me], 0, keepdims=False)
-        swap = (own_rows[:, None] == jnp.arange(ROWS, dtype=jnp.int32)[None, :]).astype(BF16)
-        cut_block = jnp.dot(swap, master.reshape(ROWS, 1024).astype(BF16), preferred_element_type=F32).astype(BF16)
+        cut_block = cut_owned(own_rows[:, None], master.reshape(-1, 128))
         levels = jnp.zeros((8, 128), jnp.int32).at[:4, :4].set(noise_levels)
         cut, all_levels, tok, cot = scatter_blocks(cut_block, levels, tokens, out_cotangent, total, batch_size)
         ordered = pick_blocks(inverse, cut)
@@ -850,8 +1147,6 @@
         mod_part = jnp.dot(
             cond_all, ordered[: FIRST + 1].reshape(-1, 128), preferred_element_type=F32
         ).reshape(16, 24, 128)
-        w_qkv, w_out, w_in, w_down, mod_parts = gather_matrices(held, mod_part, total, batch_size)
-        modulation = jnp.sum(mod_parts, axis=0).reshape(6, 4, width).transpose(1, 0, 2)
     else:
         tok, cot = swap_videos([tokens, out_cotangent], videos, per, 0)
         gathered = lax.all_gather(master.astype(BF16), ("frame", "batch"), axis=0, tiled=True)
@@ -865,8 +1160,6 @@
     piece_frame = piece_at // frame_len
     ends = (piece_frame + 1) * frame_len
     selector = (piece_frame[:, None] == jnp.arange(frame_count, dtype=jnp.int32)[None, :]).astype(F32)
-    piece_mod = jnp.einsum("pf,fjd->jpd", selector, modulation, precision=HIGHEST)
-    shift_one, scale_one, gate_one, shift_two, scale_two, gate_two = [piece_mod[j][:, None, :] for j in range(6)]
 
     def flat(a):
         return a.reshape(rows, a.shape[-1])
@@ -874,39 +1167,59 @@
     def cube(a):
         return a.reshape(videos, piece, a.shape[-1])
 
+    def partners(k):
+        return [(i, i // per * per + (i + k) % per) for i in range(frame_size)]
+
+    def split_mod(piece_mod):
+        return [piece_mod[j][:, None, :] for j in range(6)]
+
     x_float = tok.astype(F32)
     normed_one, inv_one = layer_stats(x_float)
-    h_one = flat((normed_one * (1.0 + scale_one) + shift_one).astype(BF16))
-    projected = jnp.dot(h_one, w_qkv, preferred_element_type=F32)
-    queries = (projected[:, :width] * q_scale).astype(BF16)
-    kv_own = projected[:, width:].astype(BF16)
-
-    def partners(k):
-        return [(i, i // per * per + (i + k) % per) for i in range(frame_size)]
-
-    kv_all = jnp.zeros((per, rows, 2 * width), BF16)
-    kv_all = lax.dynamic_update_index_in_dim(kv_all, kv_own, g, 0)
-    for k in range(1, per):
-        kv_all = lax.dynamic_update_index_in_dim(
-            kv_all, lax.ppermute(kv_own, "frame", partners(k)), (g + per - k) % per, 0
+    if direct:
+        (
+            w_qkv, w_out, w_in, w_down, h_one, queries, kv_all, attended,
+            attn_out, middle, h_two, slope, act_low, mlp_out, block_output, piece_mod,
+        ) = forward(selector, ends, tok.reshape(rows, width), held, mod_part, total, batch_size, piece, per)
+        kv_all = kv_all.reshape(keys, 2 * width)
+        middle = cube(middle)
+        block_output = cube(block_output)
+        normed_two, inv_two = layer_stats(middle)
+        shift_one, scale_one, gate_one, shift_two, scale_two, gate_two = split_mod(
+            piece_mod.reshape(6, videos, width)
         )
-    kv_all = kv_all.reshape(keys, 2 * width)
-    attended = attend(ends, queries, kv_all, piece, per)
-    attn_out = jnp.dot(attended, w_out, preferred_element_type=F32)
-    middle = x_float + gate_one * cube(attn_out)
-    normed_two, inv_two = layer_stats(middle)
-    h_two = flat((normed_two * (1.0 + scale_two) + shift_two).astype(BF16))
-    pre_act = jnp.dot(h_two, w_in, preferred_element_type=F32)
-    activated, gelu_back = jax.vjp(partial(jax.nn.gelu, approximate=True), pre_act)
-    act_low = activated.astype(BF16)
-    mlp_out = jnp.dot(act_low, w_down, preferred_element_type=F32)
-    block_output = (middle + gate_two * cube(mlp_out)).astype(BF16)
+    else:
+        piece_mod = jnp.einsum("pf,fjd->jpd", selector, modulation, precision=HIGHEST)
+        shift_one, scale_one, gate_one, shift_two, scale_two, gate_two = split_mod(piece_mod)
+
+        h_one = flat((normed_one * (1.0 + scale_one) + shift_one).astype(BF16))
+        projected = jnp.dot(h_one, w_qkv, preferred_element_type=F32)
+        queries = (projected[:, :width] * q_scale).astype(BF16)
+        kv_own = projected[:, width:].astype(BF16)
+
+        kv_all = jnp.zeros((per, rows, 2 * width), BF16)
+        kv_all = lax.dynamic_update_index_in_dim(kv_all, kv_own, g, 0)
+        for k in range(1, per):
+            kv_all = lax.dynamic_update_index_in_dim(
+                kv_all, lax.ppermute(kv_own, "frame", partners(k)), (g + per - k) % per, 0
+            )
+        kv_all = kv_all.reshape(keys, 2 * width)
+        attended = attend(ends, queries, kv_all, piece, per)
+        attn_out = jnp.dot(attended, w_out, preferred_element_type=F32)
+        middle = x_float + gate_one * cube(attn_out)
+        normed_two, inv_two = layer_stats(middle)
+        h_two = flat((normed_two * (1.0 + scale_two) + shift_two).astype(BF16))
+        pre_act = jnp.dot(h_two, w_in, preferred_element_type=F32)
+        activated, gelu_back = jax.vjp(partial(jax.nn.gelu, approximate=True), pre_act)
+        act_low = activated.astype(BF16)
+        slope = gelu_back(jnp.ones_like(pre_act))[0]
+        mlp_out = jnp.dot(act_low, w_down, preferred_element_type=F32)
+        block_output = (middle + gate_two * cube(mlp_out)).astype(BF16)
 
     grad_out = cot.astype(F32)
     d_mlp = flat((gate_two * grad_out).astype(BF16))
     g_down = jnp.dot(act_low.T, d_mlp, preferred_element_type=F32).astype(BF16)
     d_act = jnp.dot(d_mlp, w_down.T, preferred_element_type=F32)
-    d_pre = gelu_back(d_act)[0].astype(BF16)
+    d_pre = (d_act * slope.astype(F32)).astype(BF16)
     g_in = jnp.dot(h_two.T, d_pre, preferred_element_type=F32).astype(BF16)
     d_htwo = cube(jnp.dot(d_pre, w_in.T, preferred_element_type=F32))
     d_gate_two = jnp.sum(grad_out * cube(mlp_out), axis=1)
@@ -945,9 +1258,14 @@
         ordered_grad = jnp.concatenate([ada_grad[: FIRST * GROUP], edge, held_grad[GROUP:]], axis=0)
         cut_grad = pick_blocks(owned_block, ordered_grad.reshape(total, GROUP, 128))
         grad_block, outputs, input_grads = collect_blocks(cut_grad, block_output, input_grad, total, batch_size)
-        shard_total = lax.dot_general(
-            swap, grad_block, (((0,), (0,)), ((), ())), preferred_element_type=F32
-        ).reshape(1, block_size)
+        updated = update_owned(
+            own_rows[None, :],
+            grad_block,
+            master.reshape(-1, 128),
+            first_moment.reshape(-1, 128),
+            second_moment.reshape(-1, 128),
+        )
+        new_master, new_first, new_second = [a.reshape(1, block_size) for a in updated]
     else:
         outputs, input_grads = swap_videos([block_output, input_grad], videos, per, 1)
         g_ada = lax.dot_general(
@@ -963,12 +1281,7 @@
         shard_total = lax.psum_scatter(
             arranged, ("frame", "batch"), scatter_dimension=0, tiled=True
         ).reshape(1, block_size)
-    new_first = BETA_ONE * first_moment + (1.0 - BETA_ONE) * shard_total
-    new_second = BETA_TWO * second_moment + (1.0 - BETA_TWO) * shard_total * shard_total
-    fix_one = 1.0 - BETA_ONE**STEP
-    fix_two = 1.0 - BETA_TWO**STEP
-    update = new_first / fix_one / (jnp.sqrt(new_second / fix_two) + ADAM_EPS)
-    new_master = master - LEARN_RATE * (update + WEIGHT_DECAY * master)
+        new_master, new_first, new_second = adam(shard_total, master, first_moment, second_moment)
     return (outputs, input_grads, new_master, new_first, new_second)
 
 

time: 665 us -> 565 us (0.85)
  matrix products: 98.6 us -> 55.2 us
  other arithmetic: 66.2 us -> 27.9 us
  Pallas kernels: 458 us -> 447 us
  local copies, waits for them, and re-layouts: 28.3 us -> 19.8 us
    dot_general x7 -> x0, matrix products: 38.5 us -> none  [the longest x1 15.8 us: shards(): pre_act = jnp.dot(h_two, w_in, preferred_element_type=F32)]
    convert_element_type x4 -> x1, other arithmetic: 30.1 us -> 0.65 us  [shards(): (piece_frame[:, None] == jnp.arange(frame_count, dtype=jnp.int32)[None, :...]
    sub x1 -> x0, other arithmetic: 18.3 us -> none  [shards(): new_master = master - LEARN_RATE * (update + WEIGHT_DECAY * master)]
    pallas_call x2 -> x3, Pallas kernels: 176 us -> 170 us  [the longest x1 156 us: forward(): pl.pallas_call(partial(forward_kernel_entry, total, batch, piece, per), o...]
  transfers between devices with their start and end apart: 2 -> 1, of which waited for: 0 -> 0; matrix products, arithmetic and copies ran while one was open for 4% -> 4% of each run, Pallas kernels for 0% -> 0%
where the time goes in v2:
time: 565 us; the launch traced here: 555 us
  Pallas kernels  447 us (79%)
  matrix products  55.2 us (10%)
  other arithmetic  27.9 us (5%)
  local copies, waits for them, and re-layouts  19.8 us (4%)
    pallas_call x1, Pallas kernels, forward(): pl.pallas_call(partial(forward_kernel_entry, total, batch, piece, per), o...  156 us
    pallas_call x1, Pallas kernels, reduce_matrices(): pl.pallas_call(partial(reduce_kernel, total, batch), out_shape=[jax.Shape...  145 us
    pallas_call x1, Pallas kernels, scatter_blocks(): pl.pallas_call(partial(scatter_kernel, total, batch), out_shape=[jax.Shap...  45.3 us
    pallas_call x1, Pallas kernels, collect_blocks(): pl.pallas_call(partial(collect_kernel, total, batch), out_shape=[jax.Shap...  44.8 us
    pallas_call x1, Pallas kernels, attend_back(): pl.pallas_call(partial(attend_back_kernel, piece, per), grid_spec=pltpu.P...  37.8 us
    dot_general x1, matrix products, shards(): d_act = jnp.dot(d_mlp, w_down.T, preferred_element_type=F32)  11.8 us
  transfers between devices with their start and end apart: 1, of which 0 were waited for; matrix products, arithmetic and copies ran while one was open for 4% of the time, Pallas kernels for 0%

profile of v2, /device:TPU:0, one launch (start us, length us, event | category | flops | bytes accessed | tf_op | source)
XLA Modules:
  0.0 554.9 jit_solution(3112849609320387980)
XLA Ops:
  7.3 2.3 sort.17
  9.6 4.6 cut_owned.1.blk
  14.2 45.3 %scatter_blocks.1 = (bf16[32,144,128]{2,1,0:T(8,128)(2,1)}, s32[4,8,128]{2,1,0:T(8,128)}, bf16[4,128,1024]{2,1,0:T(8,128)(2,1)}, bf16[4,128,1024]{2,1,0:T(8,128)(2,1)}) custom-call(bf16[576,1024]{1,0:T(8,128)(2,1)} %cut_owned.1.blk, s32[8,128]{1,0:T(8,128)} %scatter.4.levels, bf16[4,128,1024]{2,1,0:T(8,128)(2,1)} %tok.1, bf16[4,128,1024]{2,1,0:T(8,128)(2,1)} %cot.1), custom_call_target="tpu_custom_call" | custom-call | tf_op jit(solution)/shard_map/scatter_blocks/pallas_call | solution.py:204
  59.6 2.5 pick_blocks.2
  62.1 2.1 slice.64
  71.7 155.9 %forward.1 = (bf16[1024,3072]{1,0:T(8,128)(2,1)}, bf16[1024,1024]{1,0:T(8,128)(2,1)}, bf16[1024,4096]{1,0:T(8,128)(2,1)}, bf16[4096,1024]{1,0:T(8,128)(2,1)}, bf...) custom-call(f32[4,4]{1,0:T(4,128)} %fusion.24.sel, ...), custom_call_target="tpu_custom_call" | custom-call | tf_op jit(solution)/shard_map/forward/pallas_call | solution.py:643
  232.8 11.8 %multiply_convert_fusion = bf16[512,4096]{1,0:T(8,128)(2,1)} fusion(bf16[512,4096]{1,0:T(8,128)(2,1)} %get-tuple-element.60, bf16[512,1024]{1,0:T(8,128)(2,1)} %bitcast.119, bf16[4096,1024]{1,0:T(8,128)(2,1)} %get-tuple-element.59), kind=kOutput, calls=%fused_computation | convolution fusion | flops 4301258752 | bytes 17825792 | tf_op jit(solution)/shard_map/dot_general | solution.py:1221
  244.7 6.9 %fusion.21 = (f32[512]{0:T(512)S(1)}, f32[512]{0:T(512)S(1)}, f32[512,1024]{1,0:T(8,128)S(1)}) fusion(f32[4,1024]{1,0:T(4,128)S(1)} %get-tuple-element.94, f32[512]{0:T(512)S(1)} %get-tuple-element.104, f32[512,1024]{1,0:T(8,128)S(1)} %copy-done, f32[512]{0:T(512)S(1)} %get-tuple-element.106, bf16[512,4096]{1,0:T(8,128)(2,1)} %multiply_convert_fusion, ...), kind=kOutput, calls=%fused_computation.46 | convolution fusion | flops 4298112000 | bytes 16801792 | tf_op jit(solution)/shard_map/dot_general | solution.py:1224
  255.8 2.3 convolution_convert_fusion.4.do
  258.1 37.8 %attend_back.1 = (bf16[512,1024]{1,0:T(8,128)(2,1)}, bf16[1024,1024]{1,0:T(8,128)(2,1)}, bf16[1024,1024]{1,0:T(8,128)(2,1)}) custom-call(s32[4]{0:T(128)} %get-tuple-element.90.ends, bf16[512,1024]{1,0:T(8,128)(2,1)} %get-tuple-element.54.q, bf16[1024,2048]{1,0:T(8,128)(2,1)} %bitcast.124, bf16[1024,2048]{1,0:T(8,128)(2,1)} %bitcast.125, ...), custom_call_target="tpu_custom_call" | custom-call | flops 5368709120 | bytes 9437184 | tf_op jit(solution)/shard_map/attend_back/pallas_call | solution.py:1043
  295.9 4.8 pad_maximum_fusion
  300.7 3.2 dynamic-slice_bitcast_fusion
  306.0 2.4 broadcast_multiply_fusion.1
  308.9 2.6 convolution_convert_fusion.3.refs_1_
  311.5 9.1 %convolution_convert_fusion.1.refs_2_ = bf16[1024,4096]{1,0:T(8,128)(2,1)} fusion(bf16[512,1024]{1,0:T(8,128)(2,1)S(1)} %copy-done.18, bf16[512,4096]{1,0:T(8,128)(2,1)} %multiply_convert_fusion), kind=kOutput, calls=%fused_computation.2 | convolution fusion | flops 4299161600 | bytes 13631488 | tf_op jit(solution)/shard_map/dot_general | solution.py:1223
  320.6 6.9 %convolution_convert_fusion.refs_3_ = bf16[4096,1024]{1,0:T(8,128)(2,1)} fusion(bf16[512,4096]{1,0:T(8,128)(2,1)S(1)} %copy-done.16, bf16[512,1024]{1,0:T(8,128)(2,1)S(1)} %bitcast.120), kind=kOutput, calls=%fused_computation.1 | convolution fusion | flops 4299161600 | bytes 13631488 | tf_op jit(solution)/shard_map/dot_general | solution.py:1220
  327.6 2.5 fusion.1
  330.1 3.4 bitcast_multiply_fusion.1
  335.9 7.7 %convolution_convert_fusion.2.refs_0_ = bf16[1024,3072]{1,0:T(8,128)(2,1)} fusion(bf16[512,1024]{1,0:T(8,128)(2,1)} %get-tuple-element.53, bf16[512,2048]{1,0:T(8,128)(2,1)S(1)} %fusion.1, bf16[512,1024]{1,0:T(8,128)(2,1)} %broadcast_multiply_fusion.1), kind=kOutput, calls=%fused_computation.5 | convolution fusion | flops 3230662656 | bytes 10485760 | tf_op jit(solution)/shard_map/dot_general | solution.py:1240
  343.6 144.7 %reduce_matrices.1 = (bf16[3168,128]{1,0:T(8,128)(2,1)}, f32[32,24,128]{2,1,0:T(8,128)}) custom-call(bf16[1024,3072]{1,0:T(8,128)(2,1)} %convolution_convert_fusion.2.refs_0_, bf16[1024,1024]{1,0:T(8,128)(2,1)} %convolution_convert_fusion.3.refs_1_, bf16[1024,4096]{1,0:T(8,128)(2,1)} %convolution_convert_fusion.1.refs_2_, ...), custom_call_target="tpu_custom_call" | custom-call | tf_op jit(solution)/shard_map/reduce_matrices/pallas_call | solution.py:856
  492.2 2.6 pick_blocks.3.cut
  494.8 3.2 fusion.14.grad
  498.0 44.8 %collect_blocks.1 = (bf16[576,1024]{1,0:T(8,128)(2,1)}, bf16[4,128,1024]{2,1,0:T(8,128)(2,1)}, bf16[4,128,1024]{2,1,0:T(8,128)(2,1)}) custom-call(bf16[32,144,128]{2,1,0:T(8,128)(2,1)} %pick_blocks.3.cut, bf16[4,128,1024]{2,1,0:T(8,128)(2,1)} %bitcast.116, bf16[4,128,1024]{2,1,0:T(8,128)(2,1)} %fusion.14.grad), custom_call_target="tpu_custom_call" | custom-call | tf_op jit(solution)/shard_map/collect_blocks/pallas_call | solution.py:265
  542.8 9.0 %update_owned.1 = (f32[4608,128]{1,0:T(8,128)}, f32[4608,128]{1,0:T(8,128)}, f32[4608,128]{1,0:T(8,128)}) custom-call(s32[1,576]{1,0:T(1,128)} %get-tuple-element.97.rows, bf16[576,1024]{1,0:T(8,128)(2,1)} %get-tuple-element.77.grad, f32[4608,128]{1,0:T(8,128)} %bitcast.106, f32[4608,128]{1,0:T(8,128)} %bitcast.114, f32[4608,128]{1,0:T(8,128)} %bitcast.115), custom_call_target="tpu_custom_call" | custom-call | tf_op jit(solution)/shard_map/update_owned/pallas_call | solution.py:946
  (118 shorter events, 32.1 us)
Async XLA Ops:
  59.6 4.7 copy-start.15
  66.6 3.8 slice-start.4
  227.6 2.8 copy-start
  231.6 13.0 %slice-start = ((s8[8388608]{0:T(1024)(128)(4,1)}), s8[4194304]{0:T(1024)(128)(4,1)S(1)}, s32[]{:S(2)}) async-start(s8[8388608]{0:T(1024)(128)(4,1)} %bitcast.107), calls=%async_computation | async-start | bytes 8388608
  232.8 11.8 %slice-start.1 = ((s8[8388608]{0:T(1024)(128)(4,1)}), s8[4194304]{0:T(1024)(128)(4,1)S(1)}, s32[]{:S(2)}) async-start(s8[8388608]{0:T(1024)(128)(4,1)} %bitcast.107), calls=%async_computation.1 | async-start | bytes 8388608
  244.6 6.9 %copy-start.9 = (f32[512,1024]{1,0:T(8,128)S(1)}, f32[512,1024]{1,0:T(8,128)}, u32[]{:S(2)}) copy-start(f32[512,1024]{1,0:T(8,128)} %get-tuple-element.70) | copy-start | bytes 6291460
  244.6 6.9 %copy-start.10 = (f32[512,1024]{1,0:T(8,128)S(1)}, f32[512,1024]{1,0:T(8,128)}, u32[]{:S(2)}) copy-start(f32[512,1024]{1,0:T(8,128)} %get-tuple-element.71) | copy-start | bytes 6291460
  253.4 4.6 copy-start.2
  253.5 2.3 copy-start.17
  300.7 3.6 copy-start.1
  303.9 23.6 %collective-permute-start = (bf16[512,2048]{1,0:T(8,128)(2,1)}, bf16[512,2048]{1,0:T(8,128)(2,1)}, u32[]{:S(2)}, u32[]{:S(2)}) collective-permute-start(bf16[512,2048]{1,0:T(8,128)(2,1)} %dynamic-slice_bitcast_fusion), channel_id=1, source_target_pairs={{0,4},{4,0},{8,12},{12,8},{16,20},{20,16},{24,28},{28,24},{1,5},{5... | collective-permute-start | bytes 6291464 | tf_op jit(solution)/shard_map/ppermute | solution.py:1238
  306.0 2.8 copy-start.19
  308.8 2.6 copy-start.18
  311.5 9.1 %copy-start.11 = (bf16[4,128,1024]{2,1,0:T(8,128)(2,1)S(1)}, bf16[4,128,1024]{2,1,0:T(8,128)(2,1)}, u32[]{:S(2)}) copy-start(bf16[4,128,1024]{2,1,0:T(8,128)(2,1)} %fusion.16) | copy-start | bytes 3145732
  311.5 9.1 %copy-start.16 = (bf16[512,4096]{1,0:T(8,128)(2,1)S(1)}, bf16[512,4096]{1,0:T(8,128)(2,1)}, u32[]{:S(2)}) copy-start(bf16[512,4096]{1,0:T(8,128)(2,1)} %get-tuple-element.68) | copy-start | bytes 12582916
  311.5 18.6 %slice-start.2 = ((s8[6291456]{0:T(1024)(128)(4,1)}), s8[4194304]{0:T(1024)(128)(4,1)S(1)}, s32[]{:S(2)}) async-start(s8[6291456]{0:T(1024)(128)(4,1)} %bitcast.109), calls=%async_computation.2 | async-start | bytes 8388608
  320.6 7.0 %copy-start.5 = (bf16[1024,2048]{1,0:T(8,128)(2,1)S(1)}, bf16[1024,2048]{1,0:T(8,128)(2,1)}, u32[]{:S(2)}) copy-start(bf16[1024,2048]{1,0:T(8,128)(2,1)} %pad_maximum_fusion) | copy-start | bytes 12582916
  320.6 9.5 %slice-start.3 = ((s8[6291456]{0:T(1024)(128)(4,1)}), s8[2097152]{0:T(1024)(128)(4,1)S(1)}, s32[]{:S(2)}) async-start(s8[6291456]{0:T(1024)(128)(4,1)} %bitcast.109), calls=%async_computation.3 | async-start | bytes 4194304
  327.5 2.5 copy-start.8
  343.6 145.9 %copy-start.6 = (bf16[384,1584]{1,0:T(8,128)(2,1)S(1)}, bf16[384,1584]{1,0:T(8,128)(2,1)}, u32[]{:S(2)}) copy-start(bf16[384,1584]{1,0:T(8,128)(2,1)} %mul.225) | copy-start | bytes 3649540
  488.4 2.7 copy-start.14
  491.1 3.7 copy-start.3
  542.8 9.0 %copy-start.13 = (bf16[4,128,1024]{2,1,0:T(8,128)(2,1)S(1)}, bf16[4,128,1024]{2,1,0:T(8,128)(2,1)}, u32[]{:S(2)}) copy-start(bf16[4,128,1024]{2,1,0:T(8,128)(2,1)} %get-tuple-element.127) | copy-start | bytes 3145732
  551.9 1.6 copy-start.12
  (3 other events, 3.8 us)

commit v3 on v2

--- a/solution.py
+++ b/solution.py
@@ -225,7 +225,7 @@
     )(blk, levels, tok, cot)
 
 
-def collect_kernel(total, batch, cut, act, grad, blk, act_out, grad_out, send, recv, vsend, vrecv, own):
+def collect_kernel(total, batch, cut, grad, blk, grad_out, send, recv, vsend, vrecv, own):
     f, z = frame_index()
     me = f * batch + z
     greet_all(total, batch)
@@ -251,7 +251,7 @@
 
     lax.fori_loop(1, total, lambda k, c: (group(k, True), c)[1], 0)
     copies = [local(cut.at[me], spot(f, z), own.at[0])]
-    for a, (src, dst) in enumerate(((act, act_out), (grad, grad_out))):
+    for a, (src, dst) in enumerate(((grad, grad_out),)):
         for k in range(1, 4):
             v = (mine + k) % 4
             copies.append(remote(src.at[v], dst.at[mine], vsend.at[a, k], vrecv.at[a, k], (v * 2 + g, z)))
@@ -261,16 +261,15 @@
     lax.fori_loop(1, total, lambda k, c: (group(k, False), c)[1], 0)
 
 
-def collect_blocks(cut, act, grad, total, batch):
+def collect_blocks(cut, grad, total, batch):
     return pl.pallas_call(
         partial(collect_kernel, total, batch),
         out_shape=[
             jax.ShapeDtypeStruct((ROWS, 1024), BF16),
-            jax.ShapeDtypeStruct(act.shape, act.dtype),
             jax.ShapeDtypeStruct(grad.shape, grad.dtype),
         ],
-        in_specs=[ANY] * 3,
-        out_specs=[ANY] * 3,
+        in_specs=[ANY] * 2,
+        out_specs=[ANY] * 2,
         scratch_shapes=[
             pltpu.SemaphoreType.DMA((total,)),
             pltpu.SemaphoreType.DMA((total,)),
@@ -280,7 +279,7 @@
         ],
         compiler_params=pltpu.CompilerParams(collective_id=3, has_side_effects=True),
         name="collect_blocks",
-    )(cut, act, grad)
+    )(cut, grad)
 
 
 def plane():
@@ -300,9 +299,8 @@
     [("qkv", 0, 1024, 1024 * j) for j in range(3)]
     + [("out", 0, 1024, 0)]
     + [("in", 0, 1024, 1024 * j) for j in range(4)]
-    + [("down", 0, 1216, 0), ("down", 1216, 1152, 0), ("down", 2368, 1152, 0), ("down", 3520, 576, 0)]
+    + [("down", 1024 * n, 1024, 0) for n in range(4)]
 )
-DOWN_READY = (1152, 2304, 3456, 4096)
 DEALS = (
     [("qkv", j, 0, 1024) for j in range(3)]
     + [("out", 0, 0, 1024), ("in", None, 0, 1024)]
@@ -344,10 +342,64 @@
     return centre * inv_std, inv_std
 
 
-def forward_kernel(total, batch, piece, per, sel, ends, tok, held, mod, *refs):
-    hbm, vm, sems = refs[:17], refs[17:33], refs[33:]
-    wq_o, wo_o, wi_o, wd_o, h1_o, q_o, kv_o, att_o, a_o, x1_o, h2_o, gp_o, u_o, m_o, y_o, pm_o, mod_in = hbm
-    wq, wo, wi, wd, h1, q, kv, att, a, x1, h2, gp, u, m, pm, mod_v = vm
+def lane_half(e):
+    return lax.broadcasted_iota(jnp.int32, (1, 128), 1) // 64 == e
+
+
+def choose(mask, one, other):
+    return jnp.where(mask, one.astype(F32), other.astype(F32)).astype(BF16)
+
+
+def three_parts(value):
+    high = value.astype(BF16).astype(F32)
+    rest = value - high
+    middle = rest.astype(BF16).astype(F32)
+    return high, middle, rest - middle
+
+
+def in_lanes(parts, first):
+    lane = lax.broadcasted_iota(jnp.int32, (1, 128), 1) % 64
+    total = 0.0
+    for n, part in enumerate(parts):
+        total = total + jnp.where(lane == first + n, part, 0.0)
+    return total
+
+
+def query_mask(ends, piece):
+    lane = lax.broadcasted_iota(jnp.int32, (piece, 128), 1) % 64
+    found = []
+    for t in range(4):
+        hidden = (lane < 4) & (lane * FRAME_LO >= ends[t])
+        found.append(jnp.where(hidden, NEG_FILL, 0.0))
+    return jnp.concatenate(found, axis=0)
+
+
+def key_mask(keys, piece, per):
+    lane = lax.broadcasted_iota(jnp.int32, (keys, 128), 1) % 64
+    quarter = key_positions(keys, piece, per) // FRAME_LO
+    return jnp.where((lane == quarter) | ((lane >= 4) & (lane < 7)), 1.0, 0.0)
+
+
+def dot_nt(a, b):
+    return lax.dot_general(a, b, (((1,), (1,)), ((), ())), preferred_element_type=F32)
+
+
+def dot_tn(a, b):
+    return lax.dot_general(a, b, (((0,), (0,)), ((), ())), preferred_element_type=F32)
+
+
+def dot_nn(a, b):
+    return jnp.dot(a, b, preferred_element_type=F32)
+
+
+def fold_rows(values):
+    return values[:8] + values[8:]
+
+
+def forward_kernel(total, batch, piece, per, sel, ends, tok, cot, held, mod, *refs):
+    hbm, vm, sems = refs[:17], refs[17:36], refs[36:]
+    wq_o, wo_o, wi_o, wd_o, h1_o, q_o, qb_o, kv_o, att_o, a_o, x1_o, h2_o, gp_o, u_o, y_o, pm_o, dg_o = hbm
+    wq, wo, wi, wd, h1, q, qb, kv, att, a, x1, h2, gp, u, acc, pm, mod_v, dg, kmask = vm
     zsend, zrecv, psend, precv, msend, mrecv, own, wsem, osem, kvsend, kvrecv = sems
     mats = {"qkv": wq, "out": wo, "in": wi, "down": wd}
     mats_o = {"qkv": wq_o, "out": wo_o, "in": wi_o, "down": wd_o}
@@ -490,6 +542,7 @@
 
         row_loop(piece, step, one)
     save(h1, h1_o, 1)
+    saves_h1 = saves[-1]
 
     pump_to(4)
     for j in range(3):
@@ -511,36 +564,40 @@
     save(kv, kv_o, 3)
 
     keys = 2 * 4 * piece
-    end_of = [ends[t] for t in range(4)]
+    qb_mask = query_mask([ends[t] for t in range(4)], piece)
+    acc[:, 0:128] = qb_mask
+    kmask[...] = key_mask(keys, piece, per).astype(BF16)
 
     def heads(h):
-        outs = []
+        pair = lanes(128 * h, 128)
+        k_pair = kv[:, :, pair].reshape(keys, 128)
+        v_pair = kv[:, :, lanes(1024 + 128 * h, 128)].reshape(keys, 128)
+        q_pair = q[:, pair]
+        outs, parts = [], []
         for e in range(2):
-            def part(ref_cols):
-                return lanes(ref_cols, 128)
-
-            k_pair = kv[:, :, part(128 * h)].reshape(keys, 128)
-            v_pair = kv[:, :, part(1024 + 128 * h)].reshape(keys, 128)
-            q_pair = q[:, part(128 * h)]
-            cut = slice(64 * e, 64 * e + 64)
-            s = scores_t(k_pair[:, cut], q_pair[:, cut], end_of, piece, per)
-            peak = jnp.max(s, axis=0, keepdims=True)
-            w = jnp.exp(s - peak)
-            prob = (w * (1.0 / jnp.sum(w, axis=0, keepdims=True))).astype(BF16)
-            outs.append(
-                lax.dot_general(prob, v_pair[:, cut], (((0,), (0,)), ((), ())), preferred_element_type=F32)
-            )
-        att[:, lanes(128 * h, 128)] = jnp.concatenate(outs, axis=1).astype(BF16)
+            mine = lane_half(e)
+            s = dot_nt(choose(mine, q_pair, acc[:, 0:128]), choose(mine, k_pair, kmask[...]))
+            peak = jnp.max(s, axis=1, keepdims=True)
+            w = jnp.exp(s - peak).astype(BF16)
+            o = dot_nn(w, choose(mine, v_pair, jnp.ones_like(v_pair)))
+            outs.append(o / pltpu.roll(o, 64, 1))
+            parts.append(-(peak + jnp.log(jnp.where(mine, 1.0, o))))
+        att[:, pair] = choose(lane_half(0), outs[0], outs[1])
+        level = jnp.where(lane_half(1), parts[0], parts[1])
+        qb[:, pair] = (acc[:, 0:128] + in_lanes(three_parts(level), 4)).astype(BF16)
 
     for n in range(4):
         lax.fori_loop(2 * n, 2 * n + 2, lambda h, t: (heads(h), t)[1], 0)
         pump_to(7 + n)
     save(att, att_o, 4)
+    save(qb, qb_o, 12)
 
     ready(3)
 
     def out_cols(n):
-        a[:, lanes(n, 512)] = jnp.dot(att[...], wo[:, lanes(n, 512)], preferred_element_type=F32)
+        value = dot_nn(att[...], wo[:, lanes(n, 512)])
+        acc[:, lanes(n, 512)] = value
+        a[:, lanes(n, 512)] = value.astype(BF16)
 
     row_loop(1024, 512, out_cols)
     save(a, a_o, 5)
@@ -549,7 +606,7 @@
 
         def two(i, p=p, gate=gate, shift=shift, scale=scale):
             rows = pl.ds(pl.multiple_of(p * piece + i, step), step)
-            middle = tok[rows, :].astype(F32) + gate * a[rows, :]
+            middle = tok[rows, :].astype(F32) + gate * acc[rows, :]
             x1[rows, :] = middle
             normed, _ = norm_rows(middle)
             h2[rows, :] = (normed * (1.0 + scale) + shift).astype(BF16)
@@ -564,45 +621,42 @@
 
         def in_cols(n, j=j):
             col = 1024 * j + n
-            pre = jnp.dot(h2[...], wi[:, lanes(col, 256)], preferred_element_type=F32)
+            pre = jnp.dot(h2[...], wi[:, lanes(col, 512)], preferred_element_type=F32)
             square = pre * pre
             t = jnp.tanh(GELU_A * (pre + GELU_B * (square * pre)))
             lift = 0.5 * (1.0 + t)
-            u[:, lanes(col, 256)] = (pre * lift).astype(BF16)
+            u[:, lanes(col, 512)] = (pre * lift).astype(BF16)
             slope = lift + (0.5 * GELU_A) * pre * (1.0 - t * t) * (1.0 + 3.0 * GELU_B * square)
-            gp[:, lanes(col, 256)] = slope.astype(BF16)
-
-        row_loop(1024, 256, in_cols)
+            gp[:, lanes(col, 512)] = slope.astype(BF16)
+
+        row_loop(1024, 512, in_cols)
     save(u, u_o, 8)
     save(gp, gp_o, 9)
-    before = 0
     for n in range(4):
         ready(8 + n)
-        depth = DOWN_READY[n] - before
-
-        def down_cols(col, n=n, before=before, depth=depth):
-            part = jnp.dot(
-                u[:, pl.ds(before, depth)], wd[pl.ds(before, depth), lanes(col, 512)], preferred_element_type=F32
-            )
+
+        def down_cols(col, n=n):
+            part = dot_nn(u[:, 1024 * n : 1024 * n + 1024], wd[1024 * n : 1024 * n + 1024, lanes(col, 512)])
             if n == 0:
-                m[:, lanes(col, 512)] = part
+                acc[:, lanes(col, 512)] = part
             else:
-                m[:, lanes(col, 512)] = m[:, lanes(col, 512)] + part
+                acc[:, lanes(col, 512)] = acc[:, lanes(col, 512)] + part
 
         row_loop(1024, 512, down_cols)
-        before = DOWN_READY[n]
-    save(m, m_o, 10)
+    saves_h1.wait()
     for p in range(4):
         gate = mod_row(5, p)
 
-        def three(i, p=p, gate=gate):
-            rows = pl.ds(pl.multiple_of(p * piece + i, step), step)
-            h1[rows, :] = (x1[rows, :] + gate * m[rows, :]).astype(BF16)
-
-        if p == 0:
-            saves[1].wait()
-        row_loop(piece, step, three)
-    saves_h1 = saves[1]
+        def three(i, total_grad, p=p, gate=gate):
+            rows = pl.ds(pl.multiple_of(p * piece + i * 16, 16), 16)
+            value = acc[rows, :]
+            h1[rows, :] = (x1[rows, :] + gate * value).astype(BF16)
+            return total_grad + fold_rows(cot[rows, :].astype(F32) * value)
+
+        part = lax.fori_loop(0, piece // 16, three, jnp.zeros((8, 1024), F32))
+        dg[pl.ds(p, 1), :] = jnp.sum(part, axis=0, keepdims=True)
+    dg[pl.ds(4, 4), :] = jnp.zeros((4, 1024), F32)
+    save(dg, dg_o, 10)
     save(h1, y_o, 11)
     for copy in saves:
         if copy is not saves_h1:
@@ -616,34 +670,38 @@
             pltpu.make_async_copy(whole(d), whole(d), zsend.at[d, k]).wait()
 
 
-def forward(sel, ends, tok, held, mod, total, batch, piece, per):
+def forward(sel, ends, tok, cot, held, mod, total, batch, piece, per):
     def out(*shape, dtype=BF16):
         return jax.ShapeDtypeStruct(shape, dtype)
 
     outs = [out(depth, 1024 * blocks) for _, depth, blocks in KINDS] + [
+        out(512, 1024),
         out(512, 1024),
         out(512, 1024),
         out(2, 512, 2048),
         out(512, 1024),
-        out(512, 1024, dtype=F32),
+        out(512, 1024),
         out(512, 1024, dtype=F32),
         out(512, 1024),
         out(512, 4096),
         out(512, 4096),
-        out(512, 1024, dtype=F32),
         out(512, 1024),
         out(24, 1024, dtype=F32),
+        out(8, 1024, dtype=F32),
     ]
     bufs = [pltpu.VMEM(o.shape, o.dtype) for o in outs[:14]] + [
+        pltpu.VMEM((512, 1024), F32),
         pltpu.VMEM((24, 1024), F32),
         pltpu.VMEM((batch, 24, 1024), F32),
+        pltpu.VMEM((8, 1024), F32),
+        pltpu.VMEM((1024, 128), BF16),
     ]
     smem = pl.BlockSpec(memory_space=pltpu.SMEM)
     dma = pltpu.SemaphoreType.DMA
     return pl.pallas_call(
-        partial(forward_kernel_entry, total, batch, piece, per),
+        partial(forward_kernel, total, batch, piece, per),
         out_shape=outs,
-        in_specs=[smem, smem, pl.BlockSpec(memory_space=pltpu.VMEM), ANY, ANY],
+        in_specs=[smem, smem] + [pl.BlockSpec(memory_space=pltpu.VMEM)] * 2 + [ANY, ANY],
         out_specs=[ANY] * len(outs),
         scratch_shapes=bufs
         + [
@@ -655,7 +713,7 @@
             dma((total,)),
             dma((len(DEALS) + 1,)),
             dma((len(UNITS),)),
-            dma((12,)),
+            dma((13,)),
             dma,
             dma,
         ],
@@ -663,41 +721,395 @@
             collective_id=1, has_side_effects=True, vmem_limit_bytes=VMEM_LIMIT
         ),
         name="forward",
-    )(sel, ends, tok, held, mod)
-
-
-def forward_kernel_entry(total, batch, piece, per, sel, ends, tok, held, mod, *refs):
-    forward_kernel(total, batch, piece, per, sel, ends, tok, held, mod, *refs[:16], None, *refs[16:])
-
-
-def add_rows(dst, dst_col, src, src_col, width, first, count):
-    step = 128
-
-    def body(i, carry):
-        rows = pl.ds(pl.multiple_of(first + i * step, 16), step)
-        dst[rows, lanes(dst_col, width)] = dst[rows, lanes(dst_col, width)] + src[rows, lanes(src_col, width)]
-        return carry
-
-    lax.fori_loop(0, count // step, body, 0)
-
-
-ORDER = (3, 2, 1, 0)
-
-
-def reduce_kernel(total, batch, *refs):
-    grads, dmod, out, dmod_out = refs[:4], refs[4], refs[5], refs[6]
-    own, got, half_sum, strip_sum = refs[7:11], refs[11:15], refs[15:19], refs[19:23]
-    zgot, psend, precv, lsem, zsend, zrecv, msend, mrecv, mown = refs[23:]
+    )(sel, ends, tok, cot, held, mod)
+
+
+LEAVES = (
+    [(3, 1024 * n, 0) for n in range(4)] + [(2, 0, j) for j in range(4)] + [(1, 0, 0)] + [(0, 0, j) for j in range(3)]
+)
+DEALS_AFTER = ((), (5,), (6,), (7, 8), (), (), (), (), (3,), (0,), (1,), (2,))
+
+
+def backward_kernel(total, batch, piece, per, sel, pm, dg, *refs):
+    wq, wo, wi, wd, h1_i, q_i, qb_i, kv_i, att_i, a_i, x1_i, h2_i, gp_i, u_i, y_i, tok_i, cot_i = refs[:17]
+    out, dmod_out, grad_o, act_o = refs[17:21]
+    big1, big2, big3, wa, wb, f1, f2, s1, s2, s3, s4, kv_got, dmv, dmf, kmask, ring = refs[21:37]
+    got, half_sum, strip_sum, zgot = refs[37:41], refs[41:45], refs[45:49], refs[49]
+    psend, precv, zsend, zrecv, msend, mrecv, vsend, vrecv, xsend, xrecv, lsem, asem, bsem = refs[50:]
     y, x, c, z, at_x, at_y, at_c = plane()
     f = 4 * y + 2 * x + c
     me = f * batch + z
+
+    def load(src, dst, n):
+        return local(src, dst, lsem.at[n])
+
+    cot_l = load(cot_i, s3, 0)
+    u_l = [load(u_i.at[:, pl.ds(1024 * n, 1024)], big1.at[:, pl.ds(1024 * n, 1024)], 1 + n) for n in range(4)]
+    h2_l = load(h2_i, s2, 5)
+    gp_l = load(gp_i, big2, 6)
+    x1_l = load(x1_i, f2, 7)
+    a_l = load(a_i, s4, 8)
+    down_tiles = [wd.at[pl.ds(512 * t, 512)] for t in range(8)] + [wo.at[pl.ds(512 * t, 512)] for t in range(2)]
+    in_tiles = [wi.at[:, pl.ds(512 * t, 512)] for t in range(8)] + [wq.at[:, pl.ds(512 * t, 512)] for t in range(6)]
+    fetched = {}
+
+    def fetch(tiles, buf, sem, t):
+        if t < len(tiles):
+            fetched[id(tiles), t] = local(tiles[t], buf.at[t % 2], sem.at[t % 2])
+
+    for t in range(2):
+        fetch(down_tiles, wb, bsem, t)
+        fetch(in_tiles, wa, asem, t)
+
+    def tile(tiles, buf, t):
+        fetched[id(tiles), t].wait()
+        return buf[t % 2]
+
     greet_all(total, batch)
+    mine, g = f // per, f % per
+    videos = []
+    for k in range(1, 4):
+        v = (mine + k) % 4
+        videos.append(remote(y_i.at[v], act_o.at[mine], vsend.at[k], vrecv.at[k], (v * per + g, z)))
+    videos.append(local(y_i.at[mine], act_o.at[mine], lsem.at[9]))
+
+    slots = {}
+    counter = [0]
+
+    def push(key, src, dst, device):
+        s = counter[0]
+        counter[0] += 1
+        slots.setdefault(key, []).append(remote(src, dst, psend.at[s], precv.at[s], device))
+
+    def arrive(key):
+        for copy in slots[key]:
+            copy.wait_recv()
+
+    def emit(n, left, right):
+        m, row, j = LEAVES[n]
+        for w in range(2):
+            ring[n % 2, :, 512 * w : 512 * w + 512] = dot_tn(left, right[:, 512 * w : 512 * w + 512]).astype(BF16)
+        push(
+            (n, 0),
+            ring.at[n % 2, :, lanes(512 * (1 - c), 512)],
+            got[m].at[pl.ds(row, 1024), pl.ds(512 * j, 512)],
+            at_c,
+        )
+
+    def add_block(dst, dst_row, dst_col, src, src_row, src_col, width, count):
+        def body(i, carry):
+            to = pl.ds(pl.multiple_of(dst_row + i * 128, 128), 128)
+            at = pl.ds(pl.multiple_of(src_row + i * 128, 128), 128)
+            dst[to, lanes(dst_col, width)] = dst[to, lanes(dst_col, width)] + src[at, lanes(src_col, width)]
+            return carry
+
+        lax.fori_loop(0, count // 128, body, 0)
+
+    def step1(n):
+        m, row, j = LEAVES[n]
+        arrive((n, 0))
+        add_block(got[m], row, 512 * j, ring.at[n % 2], 0, 512 * c, 512, 1024)
+        for copy in slots[(n, 0)]:
+            copy.wait_send()
+        for yy in range(2):
+            push(
+                (n, 1),
+                got[m].at[pl.ds(row, 512), lanes(512 * j + 256 * yy + 128 * (1 - x), 128)],
+                half_sum[m].at[pl.ds(row, 512), lanes(256 * j + 128 * yy, 128)],
+                at_x,
+            )
+        push(
+            (n, 1),
+            got[m].at[pl.ds(row + 512, 512), lanes(512 * j + 256 * (1 - y), 256)],
+            half_sum[m].at[pl.ds(row + 512, 512), lanes(256 * j, 256)],
+            at_y,
+        )
+
+    def step2(n):
+        m, row, j = LEAVES[n]
+        arrive((n, 1))
+        for yy in range(2):
+            add_block(half_sum[m], row, 256 * j + 128 * yy, got[m], row, 512 * j + 256 * yy + 128 * x, 128, 512)
+        add_block(half_sum[m], row + 512, 256 * j, got[m], row + 512, 512 * j + 256 * y, 256, 512)
+        push(
+            (n, 2),
+            half_sum[m].at[pl.ds(row, 512), lanes(256 * j + 128 * (1 - y), 128)],
+            strip_sum[m].at[pl.ds(row, 512), lanes(128 * j, 128)],
+            at_y,
+        )
+        push(
+            (n, 2),
+            half_sum[m].at[pl.ds(row + 512, 512), lanes(256 * j + 128 * (1 - x), 128)],
+            strip_sum[m].at[pl.ds(row + 512, 512), lanes(128 * j, 128)],
+            at_x,
+        )
+
+    def step3(n):
+        m, row, j = LEAVES[n]
+        arrive((n, 2))
+        add_block(strip_sum[m], row, 128 * j, half_sum[m], row, 256 * j + 128 * y, 128, 512)
+        add_block(strip_sum[m], row + 512, 128 * j, half_sum[m], row + 512, 256 * j + 128 * x, 128, 512)
+        if m == 2:
+
+            @pl.when(z != j)
+            def _():
+                k = (j - z + batch) % batch
+                remote(
+                    strip_sum[m].at[:, pl.ds(128 * j, 128)],
+                    zgot.at[k - 1, pl.ds(1120, 1024)],
+                    zsend.at[4, k],
+                    zrecv.at[4, k],
+                    (f, j),
+                )
+
+        for d in DEALS_AFTER[n]:
+            for k in range(1, batch):
+                to = (z + k) % batch
+                for held_row, count, at, col in deal_pieces(d, to):
+                    remote(
+                        strip_sum[m].at[pl.ds(pl.multiple_of(at, 16), count), lanes(128 * col, 128)],
+                        zgot.at[k - 1, pl.ds(held_row, count)],
+                        zsend.at[d, k],
+                        zrecv.at[d, k],
+                        (f, to),
+                    )
+
+    def whole(d, k):
+        return zgot.at[k - 1, pl.ds(0, DEAL_ROWS[d])]
+
+    def last(d):
+        m = [kind for kind, _, _ in KINDS].index(DEALS[d][0])
+        for k in range(1, batch):
+            pltpu.make_async_copy(whole(d, k), whole(d, k), zrecv.at[d, k]).wait()
+        for row, count, at, j in deal_pieces(d, z):
+            step = 128 if count == 1024 else count
+
+            def body(i, carry, row=row, at=at, j=j, step=step):
+                rows = pl.ds(pl.multiple_of(row + i * step, 16), step)
+                value = strip_sum[m][pl.ds(pl.multiple_of(at + i * step, 16), step), lanes(128 * j, 128)]
+                value = value.astype(F32)
+                for k in range(batch - 1):
+                    value = value + zgot[k, rows, :].astype(F32)
+                out[rows, :] = value.astype(BF16)
+                return carry
+
+            lax.fori_loop(0, count // step, body, 0)
+
+    def mod_row(j, p):
+        return pm[pl.ds(4 * j + p, 1), :]
+
+    def by_rows(p, body, sums):
+        def one(i, carry):
+            return body(pl.ds(pl.multiple_of(p * piece + i * 16, 16), 16), *carry)
+
+        start = tuple(jnp.zeros((8, 1024), F32) for _ in range(sums))
+        return [jnp.sum(s, axis=0, keepdims=True) for s in lax.fori_loop(0, piece // 16, one, start)]
+
+    cot_l.wait()
+    for p in range(4):
+        gate = mod_row(5, p)
+
+        def d_mlp(rows, gate=gate):
+            s1[rows, :] = (gate * s3[rows, :].astype(F32)).astype(BF16)
+            return ()
+
+        by_rows(p, d_mlp, 0)
+        dmv[pl.ds(20 + p, 1), :] = dg[pl.ds(p, 1), :]
+    for n in range(4):
+        u_l[n].wait()
+        emit(n, big1[:, 1024 * n : 1024 * n + 1024], s1)
+        if n >= 1:
+            step1(n - 1)
+    kv_l = [load(kv_i.at[d], big1.at[:, pl.ds(2048 * d, 2048)], 10 + d) for d in range(2)]
+    gp_l.wait()
+    for t in range(8):
+        cols = slice(512 * t, 512 * t + 512)
+        d_act = dot_nt(s1[...], tile(down_tiles, wb, t))
+        big3[:, cols] = (d_act * big2[:, cols].astype(F32)).astype(BF16)
+        fetch(down_tiles, wb, bsem, t + 2)
+        if t == 0:
+            step1(3)
+        if t == 5:
+            step2(0)
+    h2_l.wait()
+    for j in range(4):
+        emit(4 + j, s2[...], big3.at[:, 1024 * j : 1024 * j + 1024])
+        if j >= 1:
+            step1(3 + j)
+        if j == 1:
+            step2(1)
+    att_l = load(att_i, s2, 5)
+    for t in range(8):
+        part = dot_nt(big3[:, 512 * t : 512 * t + 512], tile(in_tiles, wa, t))
+        f1[...] = part if t == 0 else f1[...] + part
+        fetch(in_tiles, wa, asem, t + 2)
+        if t == 0:
+            step1(7)
+        if t == 4:
+            step2(2)
+    qb_l = load(qb_i, big3.at[:, pl.ds(3072, 1024)], 6)
+    step2(3)
+
+    x1_l.wait()
+    a_l.wait()
+    for p in range(4):
+        gate, scale = mod_row(2, p), mod_row(4, p)
+
+        def back_two(rows, d_scale, d_shift, d_gate, gate=gate, scale=scale):
+            normed, inv_std = norm_rows(f2[rows, :])
+            d_h = f1[rows, :]
+            d_mid = s3[rows, :].astype(F32) + norm_back(d_h * (1.0 + scale), normed, inv_std)
+            f2[rows, :] = d_mid
+            s1[rows, :] = (gate * d_mid).astype(BF16)
+            return (
+                d_scale + fold_rows(d_h * normed),
+                d_shift + fold_rows(d_h),
+                d_gate + fold_rows(d_mid * s4[rows, :].astype(F32)),
+            )
+
+        d_scale, d_shift, d_gate = by_rows(p, back_two, 3)
+        dmv[pl.ds(16 + p, 1), :] = d_scale
+        dmv[pl.ds(12 + p, 1), :] = d_shift
+        dmv[pl.ds(8 + p, 1), :] = d_gate
+    q_l = load(q_i, s4, 8)
+    step3(0)
+
+    att_l.wait()
+    emit(8, s2[...], s1)
+    for t in range(2):
+        s3[:, 512 * t : 512 * t + 512] = dot_nt(s1[...], tile(down_tiles, wb, 8 + t)).astype(BF16)
+    h1_l = load(h1_i, wb.at[0], 7)
+    tok_l = load(tok_i, wb.at[1], 12)
+    step1(8)
+    step3(1)
+
+    keys = 2 * 4 * piece
+    kmask[...] = key_mask(keys, piece, per).astype(BF16)
+    for copy in kv_l:
+        copy.wait()
+    qb_l.wait()
+    q_l.wait()
+
+    def heads(h):
+        pair = lanes(128 * h, 128)
+        k_pair = jnp.concatenate([big1[:, lanes(2048 * d + 128 * h, 128)] for d in range(2)], axis=0)
+        v_pair = jnp.concatenate([big1[:, lanes(2048 * d + 1024 + 128 * h, 128)] for d in range(2)], axis=0)
+        dks, dvs, dqs = [], [], []
+        first = lane_half(0)
+        ones = in_lanes([1.0, 1.0, 1.0], 0)
+        for e in range(2):
+            mask = lane_half(e)
+            k_e = choose(mask, k_pair, kmask[...])
+            v_e = choose(mask, v_pair, ones)
+            dk = dv = 0.0
+            dq = []
+            for w in range(2):
+                rows = slice(256 * w, 256 * w + 256)
+                q_w, d_w, o_w = s4[rows, pair], s3[rows, pair], s2[rows, pair]
+                q_e = choose(mask, q_w, big3[rows, lanes(3072 + 128 * h, 128)])
+                dot_rows = jnp.sum(
+                    jnp.where(mask, d_w.astype(F32) * o_w.astype(F32), 0.0), axis=1, keepdims=True
+                )
+                d_e = choose(mask, d_w, in_lanes(three_parts(-dot_rows), 0))
+                prob = jnp.exp(dot_nt(k_e, q_e))
+                d_s = (prob * dot_nt(v_e, d_e)).astype(BF16)
+                dv = dv + dot_nn(prob.astype(BF16), d_w)
+                dk = dk + dot_nn(d_s, q_w)
+                dq.append(dot_tn(d_s, k_pair))
+            dks.append(dk)
+            dvs.append(dv)
+            dqs.append(jnp.concatenate(dq, axis=0))
+        dk = choose(first, dks[0], dks[1])
+        dv = choose(first, dvs[0], dvs[1])
+        big3[:, pair] = (choose(first, dqs[0], dqs[1]).astype(F32) * HD ** (-0.5)).astype(BF16)
+        for d in range(2):
+            big2[:, lanes(2048 * d + 128 * h, 128)] = dk[512 * d : 512 * d + 512]
+            big2[:, lanes(2048 * d + 1024 + 128 * h, 128)] = dv[512 * d : 512 * d + 512]
+
+    exchanges = []
+    plan = (
+        (lambda: step2(4),),
+        (lambda: step2(5), lambda: step3(2)),
+        (lambda: step2(6), lambda: step3(3)),
+        (lambda: step2(7), lambda: step3(4)),
+        (lambda: step2(8), lambda: step3(5)),
+        (lambda: step3(6),),
+        (lambda: step3(7),),
+        (),
+    )
+    for h in range(8):
+        if h % 4 == 0:
+            pass
+        lax.fori_loop(h, h + 1, lambda n, t: (heads(n), t)[1], 0)
+        if h % 4 == 3:
+            for part in range(2):
+                at = 1024 * part + 512 * (h // 4)
+                s = len(exchanges)
+                exchanges.append(
+                    remote(
+                        big2.at[:, lanes(2048 * (1 - c) + at, 512)],
+                        kv_got.at[:, pl.ds(at, 512)],
+                        xsend.at[s],
+                        xrecv.at[s],
+                        at_c,
+                    )
+                )
+        for act in plan[h]:
+            act()
+
+    h1_l.wait()
+    emit(9, wb[0], big3.at[:, 0:1024])
+    for copy in exchanges:
+        copy.wait_recv()
+    for part in range(2):
+
+        def join(i, carry, part=part):
+            rows = pl.ds(pl.multiple_of(i * 64, 64), 64)
+            value = big2[rows, lanes(2048 * c + 1024 * part, 1024)].astype(F32) + kv_got[
+                rows, 1024 * part : 1024 * part + 1024
+            ].astype(F32)
+            big3[rows, 1024 + 1024 * part : 2048 + 1024 * part] = value.astype(BF16)
+            return carry
+
+        lax.fori_loop(0, 8, join, 0)
+        emit(10 + part, wb[0], big3.at[:, 1024 + 1024 * part : 2048 + 1024 * part])
+        step1(9 + part)
+    step3(8)
+    for t in range(6):
+        part = dot_nt(big3[:, 512 * t : 512 * t + 512], tile(in_tiles, wa, 8 + t))
+        f1[...] = part if t == 0 else f1[...] + part
+        fetch(in_tiles, wa, asem, 8 + t + 2)
+        if t == 0:
+            step1(11)
+        if t == 3:
+            step2(9)
+
+    tok_l.wait()
+    for p in range(4):
+        scale = mod_row(1, p)
+
+        def back_one(rows, d_scale, d_shift, scale=scale):
+            normed, inv_std = norm_rows(wb[1, rows, :].astype(F32))
+            d_h = f1[rows, :]
+            s1[rows, :] = (f2[rows, :] + norm_back(d_h * (1.0 + scale), normed, inv_std)).astype(BF16)
+            return d_scale + fold_rows(d_h * normed), d_shift + fold_rows(d_h)
+
+        d_scale, d_shift = by_rows(p, back_one, 2)
+        dmv[pl.ds(4 + p, 1), :] = d_scale
+        dmv[pl.ds(p, 1), :] = d_shift
+    grad_l = load(s1, grad_o, 0)
+    for j in range(6):
+        for fr in range(4):
+            value = sel[0, fr] * dmv[pl.ds(4 * j, 1), :]
+            for p in range(1, 4):
+                value = value + sel[p, fr] * dmv[pl.ds(4 * j + p, 1), :]
+            dmf[pl.ds(4 * j + fr, 1), :] = value
 
     def mod_group(k, start):
         other = (me + k) % total
         of, oz = other // batch, other % batch
         copy = pltpu.make_async_remote_copy(
-            src_ref=dmod.at[:, lanes(128 * strip_of(of), 128)],
+            src_ref=dmf.at[:, lanes(128 * strip_of(of), 128)],
             dst_ref=dmod_out.at[me],
             send_sem=msend.at[k],
             recv_sem=mrecv.at[k],
@@ -709,178 +1121,85 @@
         else:
             copy.wait()
 
-    slots = {}
-    counter = [0]
-
-    def push(key, src, dst, device):
-        s = counter[0]
-        counter[0] += 1
-        slots.setdefault(key, []).append(remote(src, dst, psend.at[s], precv.at[s], device))
-
-    def arrive(key):
-        for copy in slots[key]:
-            copy.wait_recv()
-
-    def zero(m):
-        kind, depth, blocks = KINDS[m]
-        for j in range(blocks):
-            push((m, 0), grads[m].at[:, lanes(1024 * j + 512 * (1 - c), 512)], got[m].at[:, lanes(512 * j, 512)], at_c)
-        loads[m] = [
-            local(grads[m].at[:, lanes(1024 * j + 512 * c, 512)], own[m].at[:, lanes(512 * j, 512)], lsem.at[m, j])
-            for j in range(blocks)
-        ]
-
-    def first(m):
-        kind, depth, blocks = KINDS[m]
-        half = depth // 2
-        for copy in loads[m]:
-            copy.wait()
-        arrive((m, 0))
-        add_rows(own[m], 0, got[m], 0, 512 * blocks, 0, depth)
-        for j in range(blocks):
-            for yy in range(2):
-                push(
-                    (m, 1),
-                    own[m].at[pl.ds(0, half), lanes(512 * j + 256 * yy + 128 * (1 - x), 128)],
-                    half_sum[m].at[pl.ds(0, half), lanes(256 * j + 128 * yy, 128)],
-                    at_x,
-                )
-            push(
-                (m, 1),
-                own[m].at[pl.ds(half, half), lanes(512 * j + 256 * (1 - y), 256)],
-                half_sum[m].at[pl.ds(half, half), lanes(256 * j, 256)],
-                at_y,
-            )
-
-    def second(m):
-        kind, depth, blocks = KINDS[m]
-        half = depth // 2
-        arrive((m, 1))
-        for j in range(blocks):
-            for yy in range(2):
-                add_rows(half_sum[m], 256 * j + 128 * yy, own[m], 512 * j + 256 * yy + 128 * x, 128, 0, half)
-            add_rows(half_sum[m], 256 * j, own[m], 512 * j + 256 * y, 256, half, half)
-        for j in range(blocks):
-            push(
-                (m, 2),
-                half_sum[m].at[pl.ds(0, half), lanes(256 * j + 128 * (1 - y), 128)],
-                strip_sum[m].at[pl.ds(0, half), lanes(128 * j, 128)],
-                at_y,
-            )
-            push(
-                (m, 2),
-                half_sum[m].at[pl.ds(half, half), lanes(256 * j + 128 * (1 - x), 128)],
-                strip_sum[m].at[pl.ds(half, half), lanes(128 * j, 128)],
-                at_x,
-            )
-
-    def third(m):
-        kind, depth, blocks = KINDS[m]
-        half = depth // 2
-        arrive((m, 2))
-        for j in range(blocks):
-            add_rows(strip_sum[m], 128 * j, half_sum[m], 256 * j + 128 * y, 128, 0, half)
-            add_rows(strip_sum[m], 128 * j, half_sum[m], 256 * j + 128 * x, 128, half, half)
+    lax.fori_loop(1, total, lambda k, u: (mod_group(k, True), u)[1], 0)
+    mod_own = load(dmf.at[:, lanes(128 * strip_of(f), 128)], dmod_out.at[me], 1)
+
+    out[pl.ds(0, 96), :] = jnp.zeros((96, 128), BF16)
+    step2(10)
+    step3(9)
+    for d in (5, 6, 7, 8):
+        last(d)
+    step2(11)
+    step3(10)
+    last(4)
+    last(3)
+    step3(11)
+    for d in (0, 1, 2):
+        last(d)
+    for n, copies in slots.items():
+        if n[1] > 0:
+            for copy in copies:
+                copy.wait_send()
+    for d in range(len(DEALS)):
         for k in range(1, batch):
-            to = (z + k) % batch
-            for row, count, at, j in pieces(kind, to):
-                remote(
-                    strip_sum[m].at[pl.ds(pl.multiple_of(at, 16), count), lanes(128 * j, 128)],
-                    zgot.at[k - 1, pl.ds(row, count)],
-                    zsend.at[m, k],
-                    zrecv.at[m, k],
-                    (f, to),
-                )
-
-    def whole(m, k):
-        lo, hi = SPANS[KINDS[m][0]]
-        return zgot.at[k - 1, pl.ds(lo, hi - lo)]
-
-    def last(m):
-        kind, depth, blocks = KINDS[m]
-        for k in range(1, batch):
-            pltpu.make_async_copy(whole(m, k), whole(m, k), zrecv.at[m, k]).wait()
-        for row, count, at, j in pieces(kind, z):
-            step = 128 if count == 1024 else count
-
-            def body(i, carry, row=row, at=at, j=j, step=step):
-                rows = pl.ds(pl.multiple_of(row + i * step, 16), step)
-                mine = strip_sum[m][pl.ds(pl.multiple_of(at + i * step, 16), step), lanes(128 * j, 128)]
-                total_sum = mine.astype(F32)
-                for k in range(batch - 1):
-                    total_sum = total_sum + zgot[k, rows, :].astype(F32)
-                out[rows, :] = total_sum.astype(BF16)
-                return carry
-
-            lax.fori_loop(0, count // step, body, 0)
-
-    loads = {}
-    a, b, cc, d = ORDER
-    zero(a)
-    zero(b)
-    zero(cc)
-    zero(d)
-    lax.fori_loop(1, total, lambda k, u: (mod_group(k, True), u)[1], 0)
-    mod_own = local(dmod.at[:, lanes(128 * strip_of(f), 128)], dmod_out.at[me], mown)
-    out[pl.ds(0, 96), :] = jnp.zeros((96, 128), BF16)
-    first(a)
-    first(b)
-    second(a)
-    first(cc)
-    second(b)
-    third(a)
-    first(d)
-    second(cc)
-    third(b)
-    second(d)
-    last(a)
-    third(cc)
-    last(b)
-    third(d)
-    last(cc)
-    last(d)
-    for copies in slots.values():
-        for copy in copies:
-            copy.wait_send()
-    for m in range(4):
-        for k in range(1, batch):
-            pltpu.make_async_copy(whole(m, k), whole(m, k), zsend.at[m, k]).wait()
+            pltpu.make_async_copy(whole(d, k), whole(d, k), zsend.at[d, k]).wait()
+    for copy in exchanges:
+        copy.wait_send()
+    for copy in videos:
+        copy.wait()
+    grad_l.wait()
     mod_own.wait()
     lax.fori_loop(1, total, lambda k, u: (mod_group(k, False), u)[1], 0)
 
 
-def reduce_matrices(grads, dmod, total, batch):
-    def bufs(width):
+def backward(sel, pm, dg, arrays, total, batch, piece, per):
+    def sums(width):
         return [pltpu.VMEM((depth, blocks * width), BF16) for _, depth, blocks in KINDS]
 
+    def buf(*shape, dtype=BF16):
+        return pltpu.VMEM(shape, dtype)
+
+    whole = pl.BlockSpec(memory_space=pltpu.VMEM)
+    dma = pltpu.SemaphoreType.DMA
     return pl.pallas_call(
-        partial(reduce_kernel, total, batch),
+        partial(backward_kernel, total, batch, piece, per),
         out_shape=[
             jax.ShapeDtypeStruct((HELD, 128), BF16),
-            jax.ShapeDtypeStruct((total, dmod.shape[0], 128), F32),
+            jax.ShapeDtypeStruct((total, 24, 128), F32),
+            jax.ShapeDtypeStruct((512, 1024), BF16),
+            jax.ShapeDtypeStruct((4, piece, 1024), BF16),
         ],
-        in_specs=[ANY] * 5,
-        out_specs=[pl.BlockSpec(memory_space=pltpu.VMEM), ANY],
-        scratch_shapes=bufs(512)
-        + bufs(512)
-        + bufs(256)
-        + bufs(128)
+        in_specs=[pl.BlockSpec(memory_space=pltpu.SMEM), whole, whole] + [ANY] * len(arrays),
+        out_specs=[whole, ANY, ANY, ANY],
+        scratch_shapes=[buf(512, 4096) for _ in range(3)]
+        + [buf(2, 1024, 512), buf(2, 512, 1024)]
+        + [buf(512, 1024, dtype=F32) for _ in range(2)]
+        + [buf(512, 1024) for _ in range(4)]
+        + [buf(512, 2048), buf(24, 1024, dtype=F32), buf(24, 1024, dtype=F32), buf(1024, 128), buf(2, 1024, 1024)]
+        + sums(512)
+        + sums(256)
+        + sums(128)
+        + [buf(batch - 1, HELD, 128)]
         + [
-            pltpu.VMEM((batch - 1, HELD, 128), BF16),
-            pltpu.SemaphoreType.DMA((54,)),
-            pltpu.SemaphoreType.DMA((54,)),
-            pltpu.SemaphoreType.DMA((4, 4)),
-            pltpu.SemaphoreType.DMA((4, batch)),
-            pltpu.SemaphoreType.DMA((4, batch)),
-            pltpu.SemaphoreType.DMA((total,)),
-            pltpu.SemaphoreType.DMA((total,)),
-            pltpu.SemaphoreType.DMA,
+            dma((72,)),
+            dma((72,)),
+            dma((len(DEALS), batch)),
+            dma((len(DEALS), batch)),
+            dma((total,)),
+            dma((total,)),
+            dma((4,)),
+            dma((4,)),
+            dma((4,)),
+            dma((4,)),
+            dma((13,)),
+            dma((2,)),
+            dma((2,)),
         ],
         compiler_params=pltpu.CompilerParams(
             collective_id=2, has_side_effects=True, vmem_limit_bytes=VMEM_LIMIT
         ),
-        name="reduce_matrices",
-    )(*grads, dmod)
+        name="backward",
+    )(sel, pm, dg, *arrays)
 
 
 def pick_kernel(index, src, dst):
@@ -1173,21 +1492,25 @@
     def split_mod(piece_mod):
         return [piece_mod[j][:, None, :] for j in range(6)]
 
-    x_float = tok.astype(F32)
-    normed_one, inv_one = layer_stats(x_float)
     if direct:
-        (
-            w_qkv, w_out, w_in, w_down, h_one, queries, kv_all, attended,
-            attn_out, middle, h_two, slope, act_low, mlp_out, block_output, piece_mod,
-        ) = forward(selector, ends, tok.reshape(rows, width), held, mod_part, total, batch_size, piece, per)
-        kv_all = kv_all.reshape(keys, 2 * width)
-        middle = cube(middle)
-        block_output = cube(block_output)
-        normed_two, inv_two = layer_stats(middle)
-        shift_one, scale_one, gate_one, shift_two, scale_two, gate_two = split_mod(
-            piece_mod.reshape(6, videos, width)
+        saved = forward(
+            selector, ends, tok.reshape(rows, width), cot.reshape(rows, width), held, mod_part, total, batch_size, piece, per
         )
+        *saved, block_output, piece_mod, d_gate = saved
+        held_grad, dmod_parts, input_grad, outputs = backward(
+            selector,
+            piece_mod,
+            d_gate,
+            [*saved, cube(block_output), tok.reshape(rows, width), cot.reshape(rows, width)],
+            total,
+            batch_size,
+            piece,
+            per,
+        )
+        input_grad = cube(input_grad)
     else:
+        x_float = tok.astype(F32)
+        normed_one, inv_one = layer_stats(x_float)
         piece_mod = jnp.einsum("pf,fjd->jpd", selector, modulation, precision=HIGHEST)
         shift_one, scale_one, gate_one, shift_two, scale_two, gate_two = split_mod(piece_mod)
 
@@ -1215,41 +1538,38 @@
         mlp_out = jnp.dot(act_low, w_down, preferred_element_type=F32)
         block_output = (middle + gate_two * cube(mlp_out)).astype(BF16)
 
-    grad_out = cot.astype(F32)
-    d_mlp = flat((gate_two * grad_out).astype(BF16))
-    g_down = jnp.dot(act_low.T, d_mlp, preferred_element_type=F32).astype(BF16)
-    d_act = jnp.dot(d_mlp, w_down.T, preferred_element_type=F32)
-    d_pre = (d_act * slope.astype(F32)).astype(BF16)
-    g_in = jnp.dot(h_two.T, d_pre, preferred_element_type=F32).astype(BF16)
-    d_htwo = cube(jnp.dot(d_pre, w_in.T, preferred_element_type=F32))
-    d_gate_two = jnp.sum(grad_out * cube(mlp_out), axis=1)
-    d_scale_two = jnp.sum(d_htwo * normed_two, axis=1)
-    d_shift_two = jnp.sum(d_htwo, axis=1)
-    d_middle = grad_out + norm_back(d_htwo * (1.0 + scale_two), normed_two, inv_two)
-    d_attn = flat((gate_one * d_middle).astype(BF16))
-    d_gate_one = jnp.sum(d_middle * cube(attn_out), axis=1)
-    g_out = jnp.dot(attended.T, d_attn, preferred_element_type=F32).astype(BF16)
-    d_attended = jnp.dot(d_attn, w_out.T, preferred_element_type=F32).astype(BF16)
-    dq, dk, dv = attend_back(ends, queries, kv_all, d_attended, piece, per)
-    dkv = jnp.concatenate([dk, dv], axis=1).reshape(per, rows, 2 * width)
-    dkv_own = lax.dynamic_index_in_dim(dkv, g, 0, keepdims=False).astype(F32)
-    for k in range(1, per):
-        sent = lax.dynamic_index_in_dim(dkv, (g + k) % per, 0, keepdims=False)
-        dkv_own = dkv_own + lax.ppermute(sent, "frame", partners(k)).astype(F32)
-    d_proj = jnp.concatenate([dq * jnp.asarray(q_scale, BF16), dkv_own.astype(BF16)], axis=1)
-    g_qkv = jnp.dot(h_one.T, d_proj, preferred_element_type=F32).astype(BF16)
-    d_hone = cube(jnp.dot(d_proj, w_qkv.T, preferred_element_type=F32))
-    d_scale_one = jnp.sum(d_hone * normed_one, axis=1)
-    d_shift_one = jnp.sum(d_hone, axis=1)
-    d_input = d_middle + norm_back(d_hone * (1.0 + scale_one), normed_one, inv_one)
-    input_grad = d_input.astype(BF16)
-    piece_dmod = jnp.stack([d_shift_one, d_scale_one, d_gate_one, d_shift_two, d_scale_two, d_gate_two])
-    frame_dmod = jnp.einsum("pf,jpd->jfd", selector, piece_dmod, precision=HIGHEST)
+        grad_out = cot.astype(F32)
+        d_mlp = flat((gate_two * grad_out).astype(BF16))
+        g_down = jnp.dot(act_low.T, d_mlp, preferred_element_type=F32).astype(BF16)
+        d_act = jnp.dot(d_mlp, w_down.T, preferred_element_type=F32)
+        d_pre = (d_act * slope.astype(F32)).astype(BF16)
+        g_in = jnp.dot(h_two.T, d_pre, preferred_element_type=F32).astype(BF16)
+        d_htwo = cube(jnp.dot(d_pre, w_in.T, preferred_element_type=F32))
+        d_gate_two = jnp.sum(grad_out * cube(mlp_out), axis=1)
+        d_scale_two = jnp.sum(d_htwo * normed_two, axis=1)
+        d_shift_two = jnp.sum(d_htwo, axis=1)
+        d_middle = grad_out + norm_back(d_htwo * (1.0 + scale_two), normed_two, inv_two)
+        d_attn = flat((gate_one * d_middle).astype(BF16))
+        d_gate_one = jnp.sum(d_middle * cube(attn_out), axis=1)
+        g_out = jnp.dot(attended.T, d_attn, preferred_element_type=F32).astype(BF16)
+        d_attended = jnp.dot(d_attn, w_out.T, preferred_element_type=F32).astype(BF16)
+        dq, dk, dv = attend_back(ends, queries, kv_all, d_attended, piece, per)
+        dkv = jnp.concatenate([dk, dv], axis=1).reshape(per, rows, 2 * width)
+        dkv_own = lax.dynamic_index_in_dim(dkv, g, 0, keepdims=False).astype(F32)
+        for k in range(1, per):
+            sent = lax.dynamic_index_in_dim(dkv, (g + k) % per, 0, keepdims=False)
+            dkv_own = dkv_own + lax.ppermute(sent, "frame", partners(k)).astype(F32)
+        d_proj = jnp.concatenate([dq * jnp.asarray(q_scale, BF16), dkv_own.astype(BF16)], axis=1)
+        g_qkv = jnp.dot(h_one.T, d_proj, preferred_element_type=F32).astype(BF16)
+        d_hone = cube(jnp.dot(d_proj, w_qkv.T, preferred_element_type=F32))
+        d_scale_one = jnp.sum(d_hone * normed_one, axis=1)
+        d_shift_one = jnp.sum(d_hone, axis=1)
+        d_input = d_middle + norm_back(d_hone * (1.0 + scale_one), normed_one, inv_one)
+        input_grad = d_input.astype(BF16)
+        piece_dmod = jnp.stack([d_shift_one, d_scale_one, d_gate_one, d_shift_two, d_scale_two, d_gate_two])
+        frame_dmod = jnp.einsum("pf,jpd->jfd", selector, piece_dmod, precision=HIGHEST)
 
     if direct:
-        held_grad, dmod_parts = reduce_matrices(
-            [g_qkv, g_out, g_in, g_down], frame_dmod.reshape(24, width), total, batch_size
-        )
         dmod_all = jnp.sum(dmod_parts.reshape(4, 2, 4, 24, 128), axis=1).transpose(1, 0, 2, 3).reshape(384, 128)
         ada_grad = lax.dot_general(
             cond_all.astype(F32), dmod_all, (((0,), (0,)), ((), ())), precision=HIGHEST
@@ -1257,7 +1577,7 @@
         edge = jnp.concatenate([ada_grad[FIRST * GROUP : FIRST * GROUP + 96], held_grad[96:GROUP]], axis=0)
         ordered_grad = jnp.concatenate([ada_grad[: FIRST * GROUP], edge, held_grad[GROUP:]], axis=0)
         cut_grad = pick_blocks(owned_block, ordered_grad.reshape(total, GROUP, 128))
-        grad_block, outputs, input_grads = collect_blocks(cut_grad, block_output, input_grad, total, batch_size)
+        grad_block, input_grads = collect_blocks(cut_grad, input_grad, total, batch_size)
         updated = update_owned(
             own_rows[None, :],
             grad_block,

time: 565 us -> 442 us (0.78); the launches traced: 555 us -> 439 us
  matrix products: 55.2 us -> 5.46 us
  Pallas kernels: 447 us -> 408 us
  other arithmetic: 27.9 us -> 7.63 us
  local copies, waits for them, and re-layouts: 19.8 us -> 13.2 us
    dot_general x9 -> x0, matrix products: 51 us -> none  [the longest x1 11.8 us: shards(): d_act = jnp.dot(d_mlp, w_down.T, preferred_element_type=F32)]
    pallas_call x3 -> x2, Pallas kernels: 338 us -> 311 us  [the longest x1 156 us: backward(): pl.pallas_call(partial(backward_kernel, total, batch, piece, per), out_sh...]
    pallas_call x1, Pallas kernels: 44.8 us -> 32.8 us  [collect_blocks(): pl.pallas_call(partial(collect_kernel, total, batch), out_shape=[jax.Shap...]
    convert_element_type x4 -> x0, other arithmetic: 7.19 us -> none  [the longest x1 3.24 us: shards(): input_grad = d_input.astype(BF16)]
  transfers between devices with their start and end apart: 1 -> 0, of which waited for: 0 -> 0; matrix products, arithmetic and copies ran while one was open for 4% -> 0% of each run, Pallas kernels for 0% -> 0%
where the time goes in v3:
time: 442 us; the launch traced here: 439 us
  Pallas kernels  408 us (92%)
  local copies, waits for them, and re-layouts  13.2 us (3%)
  other arithmetic  7.63 us (2%)
  matrix products  5.46 us (1%)
    pallas_call x1, Pallas kernels, backward(): pl.pallas_call(partial(backward_kernel, total, batch, piece, per), out_sh...  156 us
    pallas_call x1, Pallas kernels, forward(): pl.pallas_call(partial(forward_kernel, total, batch, piece, per), out_sha...  155 us
    pallas_call x1, Pallas kernels, scatter_blocks(): pl.pallas_call(partial(scatter_kernel, total, batch), out_shape=[jax.Shap...  46.2 us
    pallas_call x1, Pallas kernels, collect_blocks(): pl.pallas_call(partial(collect_kernel, total, batch), out_shape=[jax.Shap...  32.8 us
    pallas_call x1, Pallas kernels, update_owned(): pl.pallas_call(update_kernel, grid=(ROWS // GROUP,), out_shape=[jax.Shape...  9.02 us

profile of v3, /device:TPU:0, one launch (start us, length us, event | category | flops | bytes accessed | tf_op | source)
XLA Modules:
  0.0 438.5 jit_solution(349444396185621059)
XLA Ops:
  0.7 1.2 dynamic_slice.11
  3.8 1.2 dynamic_slice.10
  6.4 2.3 sort.17
  9.5 1.3 scatter.4.levels
  10.8 1.3 constant_dynamic-slice_fusion
  12.3 0.9 copy.15.rows
  13.1 4.6 %cut_owned.1.blk = bf16[576,1024]{1,0:T(8,128)(2,1)} custom-call(s32[576,1]{1,0:T(8,128)} %copy.15.rows, f32[4608,128]{1,0:T(8,128)} %bitcast.26), custom_call_target="tpu_custom_call" | custom-call | tf_op jit(solution)/shard_map/cut_owned/pallas_call | solution.py:1233
  17.8 46.2 %scatter_blocks.1 = (bf16[32,144,128]{2,1,0:T(8,128)(2,1)}, s32[4,8,128]{2,1,0:T(8,128)}, bf16[4,128,1024]{2,1,0:T(8,128)(2,1)}, bf16[4,128,1024]{2,1,0:T(8,128)(2,1)}) custom-call(bf16[576,1024]{1,0:T(8,128)(2,1)} %cut_owned.1.blk, s32[8,128]{1,0:T(8,128)} %scatter.4.levels, bf16[4,128,1024]{2,1,0:T(8,128)(2,1)} %tok.1, bf16[4,128,1024]{2,1,0:T(8,128)(2,1)} %cot.1), custom_call_target="tpu_custom_call" | custom-call | tf_op jit(solution)/shard_map/scatter_blocks/pallas_call | solution.py:204
  63.9 0.7 slice_convert_fusion.1
  65.3 1.5 fusion.2
  67.3 2.5 pick_blocks.2
  69.9 2.1 slice.44
  72.6 1.5 mul.101
  74.1 2.5 fusion.11.mod
  76.6 155.2 %forward.1 = (bf16[1024,3072]{1,0:T(8,128)(2,1)}, bf16[1024,1024]{1,0:T(8,128)(2,1)}, bf16[1024,4096]{1,0:T(8,128)(2,1)}, bf16[4096,1024]{1,0:T(8,128)(2,1)}, bf...) custom-call(f32[4,4]{1,0:T(4,128)} %fusion.4.sel, ...), custom_call_target="tpu_custom_call" | custom-call | tf_op jit(solution)/shard_map/forward/pallas_call | solution.py:701
  231.9 155.5 %backward.1 = (bf16[3168,128]{1,0:T(8,128)(2,1)}, f32[32,24,128]{2,1,0:T(8,128)}, bf16[512,1024]{1,0:T(8,128)(2,1)}, bf16[4,128,1024]{2,1,0:T(8,128)(2,1)}) custom-call(f32[4,4]{1,0:T(4,128)} %fusion.4.sel, f32[24,1024]{1,0:T(8,128)} %get-tuple-element.53.pm, f32[8,1024]{1,0:T(8,128)} %get-tuple-element.54.dg, bf16[1024,3072]{1,0:T(8,128)(2,1)} %get-tuple-element.55.refs_0_, ...), custom_call_target="tpu_custom_call" | custom-call | tf_op jit(solution)/shard_map/backward/pallas_call | solution.py:1164
  387.4 1.1 reduce_sum.9
  388.5 1.5 fusion.12
  390.1 1.1 pad_maximum_fusion
  391.2 2.5 pick_blocks.3.cut
  393.8 32.8 %collect_blocks.1 = (bf16[576,1024]{1,0:T(8,128)(2,1)}, bf16[4,128,1024]{2,1,0:T(8,128)(2,1)}) custom-call(bf16[32,144,128]{2,1,0:T(8,128)(2,1)} %pick_blocks.3.cut, bf16[4,128,1024]{2,1,0:T(8,128)(2,1)} %bitcast.38), custom_call_target="tpu_custom_call" | custom-call | tf_op jit(solution)/shard_map/collect_blocks/pallas_call | solution.py:265
  426.6 9.0 %update_owned.1 = (f32[4608,128]{1,0:T(8,128)}, f32[4608,128]{1,0:T(8,128)}, f32[4608,128]{1,0:T(8,128)}) custom-call(s32[1,576]{1,0:T(1,128)} %get-tuple-element.81.rows, bf16[576,1024]{1,0:T(8,128)(2,1)} %get-tuple-element.75.grad, f32[4608,128]{1,0:T(8,128)} %bitcast.27, f32[4608,128]{1,0:T(8,128)} %bitcast.35, f32[4608,128]{1,0:T(8,128)} %bitcast.36), custom_call_target="tpu_custom_call" | custom-call | tf_op jit(solution)/shard_map/update_owned/pallas_call | solution.py:1265
  435.6 1.0 copy.19
  437.2 1.0 copy.20
  (31 shorter events, 4.1 us)
Async XLA Ops:
  72.6 1.5 slice-start
  387.4 2.7 copy-start.2
  426.6 9.0 %copy-start = (bf16[4,128,1024]{2,1,0:T(8,128)(2,1)S(1)}, bf16[4,128,1024]{2,1,0:T(8,128)(2,1)}, u32[]{:S(2)}) copy-start(bf16[4,128,1024]{2,1,0:T(8,128)(2,1)} %get-tuple-element.100) | copy-start | bytes 3145732
  435.6 1.6 copy-start.1
